TPU v7x, 128 devices: a whole 4x4x4 slice. The times are simulated.
128 devices in a mesh: inline: 8 (over z, core), xline: 16 (over x, y).
Axes of the slice: x: 4, y: 4, z: 4, core: 2. Of those that a mesh axis runs over, the one named last changes fastest.
Arguments:
- traces: bfloat16 [65536, 1536], P(('inline', 'xline')), may hold values from -6 to 6
- owner: int32 [65536, 1], P(('inline', 'xline')), may hold values from 0 to 127; in each aligned block of 512 rows (0 to 511, 512 to 1023, ...) at most 8 rows name the same one
- cell: int32 [65536], P(('inline', 'xline')), may hold values from 0 to 127
- shift_table: int32 [32, 1536], replicated, may hold values from 0 to 255, as said below
- weight_table: float32 [32, 1536], replicated, as said below
- gains: float32 [256], replicated, may hold values from 0.5 to 4
Outputs:
- filtered: float32 [1536, 64, 256], P('inline', 'xline')
Inputs may be any that keep to these rules, and one draw needn't show every extreme that they name: owner is inline index * 16 + xline index of a device; among the 512 traces of one device no owner is named more than 8 times, a bound that some block reaches. `shift_table`: along t the shift of a class never rises; some class reaches 255 and some class reaches 0. `weight_table`: every entry is a whole number of 64ths, below 1.
All inputs are finite; a program needn't handle non-finite values.
Results may differ from a plain program's by a relative error of at most 0.0059.
Values may be sent and summed in bfloat16 or wider, within the bound.
No kernel may reach another device: no remote copies, remote signals or barrier semaphores. Data moves between devices by JAX's collectives and lax.ppermute only.
A program may use at most 128 MiB of HBM per device.

v0:
```python
import jax
import jax.numpy as jnp
from jax import lax
from jax.sharding import PartitionSpec as P

BIL = 8
BXL = 16


def class_columns(grouped, index):
    return jnp.take(grouped, index, axis=1)


def gathered_moveout(block, shift_table, weight_table):
    rows, samples = block.shape
    classes = shift_table.shape[0]
    group = rows // classes
    grouped = block.reshape(classes, group, samples)
    times = jnp.arange(samples, dtype=jnp.int32)[None, :] + shift_table
    first = jax.vmap(class_columns)(grouped, jnp.clip(times, 0, samples - 1)).astype(jnp.float32)
    first = jnp.where((times < samples)[:, None, :], first, 0.0)
    second = jax.vmap(class_columns)(grouped, jnp.clip(times + 1, 0, samples - 1)).astype(
        jnp.float32
    )
    second = jnp.where((times + 1 < samples)[:, None, :], second, 0.0)
    weights = weight_table[:, None, :]
    result = (1.0 - weights) * first + weights * second
    return result.astype(jnp.bfloat16).reshape(rows, samples)


def crossline_filter(gains):
    count = gains.shape[0]
    index = jnp.arange(count, dtype=jnp.int32)
    phase = index[:, None] * index[None, :] % count
    table = jnp.cos(2.0 * jnp.pi * phase.astype(jnp.float32) / count)
    kernel = jnp.dot(table, gains, precision=lax.Precision.HIGHEST) / count
    spread = (index[:, None] - index[None, :]) % count
    return jnp.take(kernel, spread, axis=0).astype(jnp.bfloat16)


def shards(traces, owner, cell, shift_table, weight_table, gains):
    rows, samples = traces.shape
    n_inline = lax.axis_size("inline")
    n_xline = lax.axis_size("xline")
    devices = n_inline * n_xline
    slots = 2 * rows // devices
    moved = gathered_moveout(traces, shift_table, weight_table)
    dest = owner[:, 0]
    member = (dest[:, None] == jnp.arange(devices, dtype=jnp.int32)[None, :]).astype(jnp.int32)
    ranks = jnp.cumsum(member, axis=0)
    place = jnp.sum(ranks * member, axis=1) - 1
    position = dest * slots + place
    outgoing = jnp.zeros((devices * slots, samples), jnp.bfloat16).at[position].set(moved)
    out_cells = jnp.full((devices * slots,), -1, jnp.int32).at[position].set(cell)
    arrived, arrived_cells = (
        lax.all_to_all(
            outgoing.reshape(devices, slots, samples),
            ("inline", "xline"),
            split_axis=0,
            concat_axis=0,
            tiled=True,
        ),
        lax.all_to_all(
            out_cells.reshape(devices, slots),
            ("inline", "xline"),
            split_axis=0,
            concat_axis=0,
            tiled=True,
        ),
    )
    arrived = arrived.reshape(devices * slots, samples)
    arrived_cells = arrived_cells.reshape(devices * slots)
    tile_bins = BIL * BXL
    select = jnp.arange(tile_bins, dtype=jnp.int32)[:, None] == arrived_cells[None, :]
    sums = jnp.dot(select.astype(jnp.bfloat16), arrived, preferred_element_type=jnp.float32)
    folds = jnp.sum(select.astype(jnp.float32), axis=1)
    stack = (
        (sums / jnp.maximum(folds, 1.0)[:, None]).astype(jnp.bfloat16).reshape(BIL, BXL, samples)
    )
    slab = lax.all_to_all(
        lax.all_to_all(stack, "inline", split_axis=2, concat_axis=0, tiled=True),
        "xline",
        split_axis=0,
        concat_axis=1,
        tiled=True,
    )
    matrix = crossline_filter(gains)
    return jnp.einsum("ab,ibt->tia", matrix, slab, preferred_element_type=jnp.float32)


def solution(mesh):
    placed = (
        P(("inline", "xline"), None),
        P(("inline", "xline"), None),
        P(("inline", "xline")),
        P(),
        P(),
        P(),
    )
    return jax.shard_map(
        shards, mesh=mesh, in_specs=placed, out_specs=P("inline", "xline", None), check_vma=False
    )
```

profile of v0, /device:TPU:0, one launch (start us, length us, event | category | flops | bytes accessed | tf_op | source)
XLA Modules:
  0.0 2209.6 jit_solution(100164499088457637)
XLA Ops:
  2.8 2.6 scatter_custom_fusion
  6.2 11.1 all-to-all-start
  17.3 1.1 bitcast_or_fusion.1
  18.4 1.8 fusion.33
  20.3 8.2 copy.44
  28.4 845.9 %gather_fusion.2 = bf16[49152,16]{1,0:T(8,128)(2,1)} fusion(bf16[32,16,1536]{1,2,0:T(8,128)(2,1)} %copy.44, s32[49152]{0:T(1024)S(1)} %reshape.194), kind=kCustom, calls=%fused_computation.1.clone | custom fusion | bytes 3538944 | tf_op jit(solution)/shard_map/vmap(jit(_take))/gather | solution.py:11
  874.3 9.6 copy.47
  883.9 840.8 %gather_fusion.1 = bf16[49152,16]{1,0:T(8,128)(2,1)} fusion(bf16[32,16,1536]{1,2,0:T(8,128)(2,1)} %copy.44, s32[49152]{0:T(1024)S(1)} %reshape.189), kind=kCustom, calls=%fused_computation.clone | custom fusion | bytes 3538944 | tf_op jit(solution)/shard_map/vmap(jit(_take))/gather | solution.py:11
  1724.7 9.6 copy.45
  1734.4 4.0 add_convert_fusion
  1738.4 6.0 scatter_custom_fusion.1
  1744.3 9.8 all-to-all-start.1
  1756.6 37.9 %all-to-all-done.1 = bf16[128,8,1536]{2,1,0:T(8,128)(2,1)S(1)} async-done(((bf16[128,8,1536]{2,1,0:T(8,128)(2,1)}), bf16[128,8,1536]{2,1,0:T(8,128)(2,1)S(1)}, u32[]{:S(2)}, u32[]{:S(2)}) %all-to-all-start.1) | async-done | bytes 3145760 | tf_op jit(solution)/shard_map/all_to_all | solution.py:56
  1795.2 2.4 copy.48
  1797.6 3.9 reshape.214
  1801.6 3.5 all-to-all-start.2
  1805.0 1.7 broadcast_clamp_fusion
  1806.7 7.2 all-to-all-done.2
  1813.9 2.3 reshape.215
  1816.3 3.0 copy.50
  1819.2 4.5 all-to-all-start.3
  1823.7 1.2 fusion.15
  1825.0 382.6 %gather_fusion = bf16[65536]{0:T(1024)(128)(2,1)S(1)} fusion(bf16[256]{0:T(256)(128)(2,1)S(1)} %broadcast_multiply_fusion, s32[65536]{0:T(1024)S(1)} %copy-done.2), kind=kCustom, calls=%fused_computation.2 | custom fusion | bytes 524288 | tf_op jit(solution)/shard_map/jit(_take)/gather | solution.py:38
  2208.2 1.4 copy.53
  (37 shorter events, 7.2 us)
Async XLA Ops:
  0.0 1823.7 %copy-start = (f32[256]{0:T(256)S(1)}, f32[256]{0:T(256)}, u32[]{:S(2)}) copy-start(f32[256]{0:T(256)} %param.13) | copy-start | bytes 3076
  0.0 20.3 copy-start.1
  6.2 1738.2 %all-to-all-start = ((s32[128,1,8]{2,1,0:T(1,128)}), s32[128,1,8]{2,1,0:T(1,128)S(1)}, u32[]{:S(2)}, u32[]{:S(2)}) async-start(s32[128,1,8]{2,1,0:T(1,128)} %bitcast.7), calls=%async_computation | async-start | bytes 131072 | tf_op jit(solution)/shard_map/all_to_all | solution.py:63
  1724.7 9.6 copy-start.3
  1744.3 50.2 %all-to-all-start.1 = ((bf16[128,8,1536]{2,1,0:T(8,128)(2,1)}), bf16[128,8,1536]{2,1,0:T(8,128)(2,1)S(1)}, u32[]{:S(2)}, u32[]{:S(2)}) async-start(bf16[128,8,1536]{2,1,0:T(8,128)(2,1)} %bitcast.16), calls=%async_computation.1 | async-start | bytes 6291456 | tf_op jit(solution)/shard_map/all_to_all | solution.py:56
  1801.6 12.3 all-to-all-start.2
  1816.3 8.8 copy-start.2
  1819.2 388.5 %all-to-all-start.3 = ((bf16[64,16,192]{2,1,0:T(8,128)(2,1)}), bf16[64,16,192]{2,1,0:T(8,128)(2,1)S(1)}, u32[]{:S(2)}, u32[]{:S(2)}) async-start(bf16[64,16,192]{2,1,0:T(8,128)(2,1)} %bitcast.70), calls=%async_computation.3 | async-start | bytes 1048576 | tf_op jit(solution)/shard_map/all_to_all | solution.py:80
where the time goes:
time: 2220 us; the launch traced here: 2210 us
  local copies, waits for them, and re-layouts  2120 us (95%)
  waiting for transfers between devices  45.1 us (2%)
  starting transfers between devices  28.8 us (1%)
    gather x6, local copies, waits for them, and re-layouts, class_columns(): return jnp.take(grouped, index, axis=1)  1710 us
    gather x2, local copies, waits for them, and re-layouts, crossline_filter(): return jnp.take(kernel, spread, axis=0).astype(jnp.bfloat16)  383 us
  transfers between devices with their start and end apart: 4, of which 2 were waited for; matrix products, arithmetic and copies ran while one was open for 96% of the time, Pallas kernels for 0%

commit v1 on v0

v1 whole, which is shorter than its diff:
```python
import functools

import numpy as np
import jax
import jax.numpy as jnp
from jax import lax
from jax.experimental import pallas as pl
from jax.experimental.pallas import tpu as pltpu
from jax.sharding import PartitionSpec as P

LANES = 128
ROWS = 512
SAMPLES = 1536
CLASSES = 32
GROUP = ROWS // CLASSES
TILES = SAMPLES // LANES
N_IN = 8
N_X = 16
DEVICES = N_IN * N_X
SLOTS = 64
HALF = LANES // 2
WHOLE = tuple(3 * (i // 2) + 2 * (i % 2) for i in range(N_IN))
SHARED = tuple(3 * i + 1 for i in range(N_IN // 2))
VMEM = 60 * 1024 * 1024


def iota(shape, dim):
    return lax.broadcasted_iota(jnp.int32, shape, dim)


def moveout(tiles, x_ref, shift_ref, weight_ref, moved_ref):
    lane = iota((8, LANES), 1)

    def eight_classes(e, carry):
        tables = pl.ds(pl.multiple_of(e * 8, 8), 8)
        shifts = [shift_ref[tables, k * LANES : (k + 1) * LANES] for k in tiles]
        weights = [weight_ref[tables, k * LANES : (k + 1) * LANES] for k in tiles]
        for c in range(8):
            one_class(pl.ds(pl.multiple_of(e * 8 * GROUP + c * GROUP, GROUP), GROUP), c, shifts, weights)
        return carry

    def one_class(rows, c, shifts, weights):
        halves = {}

        def source(k, h):
            if (k, 0) not in halves:
                both = x_ref[rows, k * LANES : (k + 1) * LANES].astype(jnp.float32)
                halves[k, 0], halves[k, 1] = both[:8], both[8:]
            return halves[k, h]

        for j, k in enumerate(tiles):
            shift = jnp.broadcast_to(shifts[j][c : c + 1], (8, LANES))
            weight = jnp.broadcast_to(weights[j][c : c + 1], (8, LANES))
            rest = 1.0 - weight
            parts = []
            early = lane + shift
            picks = []
            for u in (early, early + 1):
                picks.append((u & (LANES - 1), u < LANES, u < 2 * LANES))
            for h in range(2):
                values = []
                for index, in_first, in_second in picks:
                    got = [
                        jnp.take_along_axis(source(k + n, h), index, axis=1, mode="promise_in_bounds")
                        if k + n < TILES
                        else jnp.zeros((8, LANES), jnp.float32)
                        for n in range(3)
                    ]
                    values.append(jnp.where(in_first, got[0], jnp.where(in_second, got[1], got[2])))
                parts.append(rest * values[0] + weight * values[1])
            moved_ref[rows, j * LANES : (j + 1) * LANES] = jnp.concatenate(parts, axis=0).astype(
                jnp.bfloat16
            )

    lax.fori_loop(0, CLASSES // 8, eight_classes, 0)


def slot_of_rows(owner_row):
    owners = owner_row.astype(jnp.float32)
    blocks = [owners[:, b * LANES : (b + 1) * LANES] for b in range(ROWS // LANES)]
    columns = [jnp.transpose(jnp.broadcast_to(b, (LANES, LANES))) for b in blocks]
    earlier = iota((LANES, LANES), 0) < iota((LANES, LANES), 1)
    ranks = []
    for b, block in enumerate(blocks):
        total = jnp.zeros((LANES, LANES), jnp.float32)
        for a in range(b + 1):
            same = columns[a] == block
            if a == b:
                same = same & earlier
            total = total + jnp.where(same, 1.0, 0.0)
        ranks.append(jnp.sum(total, axis=0, keepdims=True))
    rank = jnp.concatenate(ranks, axis=1).astype(jnp.int32)
    return (owner_row & (N_X - 1)) * SLOTS + (owner_row >> 4) * 8 + rank


def spread(slot, place_ref):
    for m in range(N_X * SLOTS // LANES):
        here = iota((LANES, ROWS), 0) + m * LANES == slot
        place_ref[m * LANES : (m + 1) * LANES, :] = jnp.where(here, 1.0, 0.0).astype(jnp.bfloat16)


def pack_whole_kernel(owner_ref, cell_ref, shift_ref, weight_ref, x_ref, out_ref, slot_ref, moved_ref, place_ref):
    slot = slot_of_rows(owner_ref[...])
    slot_ref[...] = slot
    spread(slot, place_ref)
    code = ((slot >> 3) & 1) * LANES + cell_ref[...] + 1
    line = (slot >> 6) * 8 + ((slot >> 4) & 3)
    held = jnp.where(iota((LANES, ROWS), 0) == line, code.astype(jnp.float32), 0.0).astype(jnp.bfloat16)
    lanes = jnp.where((iota((LANES, ROWS), 0) & 15) == (slot & 15), 1.0, 0.0).astype(jnp.bfloat16)
    codes = lax.dot_general(
        held, lanes, (((1,), (1,)), ((), ())), preferred_element_type=jnp.float32
    ).astype(jnp.bfloat16)
    for x in range(N_X):
        for i in range(N_IN):
            out_ref[i * N_X + x, SLOTS : SLOTS + 8, :] = codes[x * 8 : (x + 1) * 8]
    moveout(WHOLE, x_ref, shift_ref, weight_ref, moved_ref)

    def two_groups(m, carry):
        place = place_ref[pl.ds(pl.multiple_of(m * LANES, LANES), LANES), :]
        for n in range(0, N_IN, 2):
            result = jnp.dot(
                place, moved_ref[:, n * LANES : (n + 2) * LANES], preferred_element_type=jnp.float32
            ).astype(jnp.bfloat16)
            for i in range(n, n + 2):
                for x in range(2):
                    out_ref[i * N_X + 2 * m + x, 0:SLOTS, :] = result[
                        x * SLOTS : (x + 1) * SLOTS, (i - n) * LANES : (i - n + 1) * LANES
                    ]
        return carry

    lax.fori_loop(0, N_X // 2, two_groups, 0)


def pack_shared_kernel(slot_ref, shift_ref, weight_ref, x_ref, out_ref, moved_ref, place_ref):
    spread(slot_ref[...], place_ref)
    moveout(SHARED, x_ref, shift_ref, weight_ref, moved_ref)
    low = iota((SLOTS // 2, LANES), 1) < HALF

    def two_groups(m, carry):
        place = place_ref[pl.ds(pl.multiple_of(m * LANES, LANES), LANES), :]
        for n in range(0, len(SHARED), 2):
            result = jnp.dot(
                place, moved_ref[:, n * LANES : (n + 2) * LANES], preferred_element_type=jnp.float32
            )
            for k in range(n, n + 2):
                for x in range(2):
                    block = result[x * SLOTS : (x + 1) * SLOTS, (k - n) * LANES : (k - n + 1) * LANES]
                    first, second = block[: SLOTS // 2], block[SLOTS // 2 :]
                    even = jnp.where(low, first, pltpu.roll(second, HALF, 1))
                    odd = jnp.where(low, pltpu.roll(first, HALF, 1), second)
                    out_ref[2 * k * N_X + 2 * m + x] = even.astype(jnp.bfloat16)
                    out_ref[(2 * k + 1) * N_X + 2 * m + x] = odd.astype(jnp.bfloat16)
        return carry

    lax.fori_loop(0, N_X // 2, two_groups, 0)


def stack_kernel(whole_ref, shared_ref, out_ref, select_ref):
    bins = (iota((2 * LANES, LANES), 0) + 1).astype(jnp.float32).astype(jnp.bfloat16)
    depth = DEVICES * 16
    ones = jnp.ones((depth, LANES), jnp.bfloat16)
    lines = []
    for j in range(DEVICES // 8):
        line = jnp.zeros((8, LANES), jnp.float32)
        for g in range(8):
            mine = (iota((8, LANES), 1) >> 4) == g
            codes = whole_ref[8 * j + g, SLOTS : SLOTS + 8, :].astype(jnp.float32)
            line = jnp.where(mine, codes, line)
        lines.append(line)
    low = iota((32, LANES), 1) < HALF
    for p in range(4):
        for j in range(DEVICES // 8):
            row = jnp.broadcast_to(lines[j][p : p + 1], (16, LANES)).astype(jnp.bfloat16)
            row = jnp.concatenate([row] * 16, axis=0)
            select_ref[:, j * LANES : (j + 1) * LANES] = jnp.where(
                bins == row, jnp.bfloat16(1), jnp.bfloat16(0)
            )
        select = select_ref[...]
        full = whole_ref[:, 16 * p : 16 * p + 16, :].reshape(depth, LANES)
        q = p % 2
        half = shared_ref[:, 16 * q : 16 * q + 16, :].reshape(depth, LANES)
        sums = jnp.dot(select, jnp.concatenate([full, ones], axis=1), preferred_element_type=jnp.float32)
        fold = jnp.maximum(sums[:, LANES:], 1.0)
        mean = sums[:, :LANES] / fold
        part = jnp.dot(select, half, preferred_element_type=jnp.float32) / fold
        for x in range(4):
            rows = slice(64 * x, 64 * x + 64)
            out_ref[4 * p + x, 0:64, :] = mean[rows].astype(jnp.bfloat16)
            first, second = part[64 * x : 64 * x + 32], part[64 * x + 32 : 64 * x + 64]
            if p < 2:
                packed = jnp.where(low, first, pltpu.roll(second, HALF, 1))
            else:
                packed = jnp.where(low, pltpu.roll(first, HALF, 1), second)
            out_ref[4 * p + x, 64:96, :] = packed.astype(jnp.bfloat16)


def filter_kernel(order_ref, matrix_ref, slab_ref, out_ref):
    whole_at, shared_at = order_ref[0], order_ref[1]
    matrix = matrix_ref[...]
    count = N_X * 16

    def apply(block):
        return lax.dot_general(block, matrix, (((0,), (0,)), ((), ())), preferred_element_type=jnp.float32)

    for i in range(4):
        full = slab_ref[:, 16 * i : 16 * i + 16, :].reshape(count, LANES)
        out_ref[pl.ds(whole_at, LANES), i, :] = apply(full)
    for i in range(2):
        pair = slab_ref[:, 64 + 16 * i : 80 + 16 * i, :].reshape(count, LANES)
        both = apply(pair)
        out_ref[pl.ds(shared_at, HALF), i, :] = both[:HALF]
        out_ref[pl.ds(shared_at, HALF), i + 2, :] = both[HALF:]


def call(kernel, name, out_shape, scratch, in_specs=None):
    extra = {} if in_specs is None else {"in_specs": in_specs}
    return pl.pallas_call(
        kernel,
        out_shape=out_shape,
        scratch_shapes=scratch,
        name=name,
        compiler_params=pltpu.CompilerParams(vmem_limit_bytes=VMEM),
        **extra,
    )


def crossline_filter(gains):
    count = gains.shape[0]
    index = np.arange(count)
    phase = 2.0 * np.pi * (index[:, None] * index[None, :] % count) / count
    basis = np.concatenate([np.cos(phase), np.sin(phase)], axis=1).astype(np.float32)
    scaled = basis * jnp.concatenate([gains, gains])[None, :]
    dims = (((1,), (1,)), ((), ()))
    product = lax.dot_general(scaled, jnp.asarray(basis), dims, precision=lax.Precision.HIGHEST)
    return (product / count).astype(jnp.bfloat16)


def exchange(block, axes):
    return lax.all_to_all(block, axes, split_axis=0, concat_axis=0, tiled=True)


def shards(traces, owner, cell, shift_table, weight_table, gains):
    bf16, both = jnp.bfloat16, ("inline", "xline")
    owner_row, cell_row = owner.reshape(1, ROWS), cell.reshape(1, ROWS)
    place = pltpu.VMEM((N_X * SLOTS, ROWS), bf16)
    whole, slot = call(
        pack_whole_kernel,
        "pack_whole",
        (
            jax.ShapeDtypeStruct((DEVICES, SLOTS + 8, LANES), bf16),
            jax.ShapeDtypeStruct((1, ROWS), jnp.int32),
        ),
        [pltpu.VMEM((ROWS, len(WHOLE) * LANES), bf16), place],
    )(owner_row, cell_row, shift_table, weight_table, traces)
    whole = exchange(whole, both)
    shared = call(
        pack_shared_kernel,
        "pack_shared",
        jax.ShapeDtypeStruct((DEVICES, SLOTS // 2, LANES), bf16),
        [pltpu.VMEM((ROWS, len(SHARED) * LANES), bf16), place],
    )(slot, shift_table, weight_table, traces)
    shared = exchange(shared, both)
    matrix = crossline_filter(gains)
    stacked = call(
        stack_kernel,
        "stack",
        jax.ShapeDtypeStruct((N_X, 96, LANES), bf16),
        [pltpu.VMEM((2 * LANES, DEVICES * 16), bf16)],
    )(whole, shared)
    slab = exchange(stacked, "xline")
    odd = lax.axis_index("inline") % 2
    order = jnp.stack([odd * HALF, (1 - odd) * LANES])
    vmem = pl.BlockSpec(memory_space=pltpu.VMEM)
    return call(
        filter_kernel,
        "crossline",
        jax.ShapeDtypeStruct((SAMPLES // N_IN, 4, N_X * 16), jnp.float32),
        [],
        [pl.BlockSpec(memory_space=pltpu.SMEM), vmem, vmem],
    )(order, matrix, slab)


def solution(mesh):
    split = P(("inline", "xline"))
    placed = (P(("inline", "xline"), None), P(("inline", "xline"), None), split, P(), P(), P())
    return jax.shard_map(
        shards, mesh=mesh, in_specs=placed, out_specs=P("inline", "xline", None), check_vma=False
    )
```

time: 2220 us -> 109 us (0.05)
  local copies, waits for them, and re-layouts: 2120 us -> 2.17 us
  blocking collectives: 0 us -> 30.3 us
  Pallas kernels: 0 us -> 25.2 us
    gather x8 -> x0, local copies, waits for them, and re-layouts: 2090 us -> none  [the longest x6 1710 us: class_columns(): return jnp.take(grouped, index, axis=1)]
    all_to_all x0 -> x1, blocking collectives: none -> 30.3 us  [exchange(): return lax.all_to_all(block, axes, split_axis=0, concat_axis=0, tiled=True)]
    pallas_call x0 -> x4, Pallas kernels: none -> 25.2 us  [the longest x1 10.3 us: shards(): call(pack_whole_kernel, 'pack_whole', (jax.ShapeDtypeStruct((DEVICES, SLO...]
    all_to_all x4 -> x2, waiting for transfers between devices: 45.1 us -> 39.9 us  [exchange(): return lax.all_to_all(block, axes, split_axis=0, concat_axis=0, tiled=True)]
  transfers between devices with their start and end apart: 4 -> 2, of which waited for: 2 -> 2; matrix products, arithmetic and copies ran while one was open for 96% -> 2% of each run, Pallas kernels for 0% -> 0%
where the time goes in v1:
time: 109 us; the launch traced here: 108 us
  waiting for transfers between devices  39.9 us (37%)
  blocking collectives  30.3 us (28%)
  Pallas kernels  25.2 us (23%)
  starting transfers between devices  8.66 us (8%)
  local copies, waits for them, and re-layouts  2.17 us (2%)
  matrix products  1.28 us (1%)
    all_to_all x2, waiting for transfers between devices, exchange(): return lax.all_to_all(block, axes, split_axis=0, concat_axis=0, tiled=True)  39.9 us
    all_to_all x1, blocking collectives, exchange(): return lax.all_to_all(block, axes, split_axis=0, concat_axis=0, tiled=True)  30.3 us
    pallas_call x1, Pallas kernels, shards(): call(pack_whole_kernel, 'pack_whole', (jax.ShapeDtypeStruct((DEVICES, SLO...  10.3 us
    all_to_all x2, starting transfers between devices, exchange(): return lax.all_to_all(block, axes, split_axis=0, concat_axis=0, tiled=True)  8.66 us
    pallas_call x1, Pallas kernels, shards(): call(pack_shared_kernel, 'pack_shared', jax.ShapeDtypeStruct((DEVICES, SL...  7.27 us
    pallas_call x1, Pallas kernels, shards(): call(stack_kernel, 'stack', jax.ShapeDtypeStruct((N_X, 96, LANES), bf16),...  5.29 us
    pallas_call x1, Pallas kernels, shards(): call(filter_kernel, 'crossline', jax.ShapeDtypeStruct((SAMPLES // N_IN, 4...  2.4 us
  transfers between devices with their start and end apart: 2, of which 2 were waited for; matrix products, arithmetic and copies ran while one was open for 2% of the time, Pallas kernels for 0%

profile of v1, /device:TPU:0, one launch (start us, length us, event | category | flops | bytes accessed | tf_op | source)
XLA Modules:
  0.0 108.2 jit_solution(11652053038202052160)
XLA Ops:
  0.0 10.3 %pack_whole.1 = (bf16[128,72,128]{2,1,0:T(8,128)(2,1)}, s32[1,512]{1,0:T(1,128)}) custom-call(s32[1,512]{1,0:T(1,128)} %bitcast.5, s32[1,512]{1,0:T(1,128)} %bitcast.6, s32[32,1536]{1,0:T(8,128)} %shift_ref.3, f32[32,1536]{1,0:T(8,128)} %weight_ref.3, bf16[512,1536]{1,0:T(8,128)(2,1)} %x_ref.3), custom_call_target="tpu_custom_call" | custom-call | tf_op jit(solution)/shard_map/pack_whole/pallas_call | solution.py:246
  10.3 7.3 %pack_shared.1 = bf16[128,32,128]{2,1,0:T(8,128)(2,1)} custom-call(s32[1,512]{1,0:T(1,128)} %get-tuple-element.8.slot_ref, s32[32,1536]{1,0:T(8,128)} %shift_ref.3, f32[32,1536]{1,0:T(8,128)} %weight_ref.3, bf16[512,1536]{1,0:T(8,128)(2,1)} %x_ref.3), custom_call_target="tpu_custom_call" | custom-call | tf_op jit(solution)/shard_map/pack_shared/pallas_call | solution.py:256
  17.5 30.3 %all_to_all.15.shared_ref = bf16[128,32,128]{2,1,0:T(8,128)(2,1)} all-to-all(bf16[128,32,128]{2,1,0:T(8,128)(2,1)} %pack_shared.1), channel_id=1, replica_groups=mesh['inline'=8,'xline'=16] {'inline','xline'}, dimensions={0} | all-to-all | bytes 2097152 | tf_op jit(solution)/shard_map/all_to_all | solution.py:239
  47.8 4.7 %all-to-all-start = ((bf16[128,72,128]{2,1,0:T(8,128)(2,1)}), bf16[128,72,128]{2,1,0:T(8,128)(2,1)S(1)}, u32[]{:S(2)}, u32[]{:S(2)}) async-start(bf16[128,72,128]{2,1,0:T(8,128)(2,1)} %get-tuple-element.7), calls=%async_computation | async-start | bytes 4718592 | tf_op jit(solution)/shard_map/all_to_all | solution.py:239
  52.5 0.0 copy-start.3
  52.5 0.0 copy-start.1
  52.5 32.4 %all-to-all-done.whole_ref = bf16[128,72,128]{2,1,0:T(8,128)(2,1)S(1)} async-done(((bf16[128,72,128]{2,1,0:T(8,128)(2,1)}), bf16[128,72,128]{2,1,0:T(8,128)(2,1)S(1)}, u32[]{:S(2)}, u32[]{:S(2)}) %all-to-all-start) | async-done | bytes 2359328 | tf_op jit(solution)/shard_map/all_to_all | solution.py:239
  85.0 0.0 copy-start
  85.0 1.4 %copy-done = bf16[128,72,128]{2,1,0:T(8,128)(2,1)} copy-done((bf16[128,72,128]{2,1,0:T(8,128)(2,1)}, bf16[128,72,128]{2,1,0:T(8,128)(2,1)S(1)}, u32[]{:S(2)}) %copy-start) | copy-done | bytes 2359320
  86.4 5.3 %stack.13 = bf16[16,96,128]{2,1,0:T(8,128)(2,1)} custom-call(bf16[128,72,128]{2,1,0:T(8,128)(2,1)} %copy-done, bf16[128,32,128]{2,1,0:T(8,128)(2,1)} %all_to_all.15.shared_ref), custom_call_target="tpu_custom_call" | custom-call | tf_op jit(solution)/shard_map/stack/pallas_call | solution.py:264
  91.7 4.0 %all-to-all-start.2 = ((bf16[16,96,128]{2,1,0:T(8,128)(2,1)}), bf16[16,96,128]{2,1,0:T(8,128)(2,1)S(1)}, u32[]{:S(2)}, u32[]{:S(2)}) async-start(bf16[16,96,128]{2,1,0:T(8,128)(2,1)} %stack.13), calls=%async_computation.2 | async-start | bytes 786432 | tf_op jit(solution)/shard_map/all_to_all | solution.py:239
  95.7 0.6 pad_add_fusion.order_ref
  96.4 0.0 copy-done.3
  96.4 0.0 copy-done.1
  96.4 1.3 %fusion.matrix_ref = bf16[256,256]{1,0:T(8,128)(2,1)} fusion(f32[256,512]{1,0:T(8,128)S(1)} %copy-done.1, f32[512]{0:T(512)S(1)} %pad_maximum_fusion), kind=kOutput, calls=%fused_computation.1 | convolution fusion | flops 402915328 | bytes 657408 | tf_op jit(solution)/shard_map/dot_general | solution.py:234
  97.6 7.4 %all-to-all-done.2.slab_ref = bf16[16,96,128]{2,1,0:T(8,128)(2,1)S(1)} async-done(((bf16[16,96,128]{2,1,0:T(8,128)(2,1)}), bf16[16,96,128]{2,1,0:T(8,128)(2,1)S(1)}, u32[]{:S(2)}, u32[]{:S(2)}) %all-to-all-start.2) | async-done | bytes 393248 | tf_op jit(solution)/shard_map/all_to_all | solution.py:239
  105.1 0.0 copy-start.2
  105.1 0.7 copy-done.2
  105.8 2.4 %crossline.1 = f32[192,4,256]{2,1,0:T(4,128)} custom-call(s32[2]{0:T(128)} %pad_add_fusion.order_ref, bf16[256,256]{1,0:T(8,128)(2,1)} %fusion.matrix_ref, bf16[16,96,128]{2,1,0:T(8,128)(2,1)} %copy-done.2), custom_call_target="tpu_custom_call" | custom-call | tf_op jit(solution)/shard_map/crossline/pallas_call | solution.py:274
  (1 shorter events, 0.0 us)
Async XLA Ops:
  47.8 37.1 %all-to-all-start = ((bf16[128,72,128]{2,1,0:T(8,128)(2,1)}), bf16[128,72,128]{2,1,0:T(8,128)(2,1)S(1)}, u32[]{:S(2)}, u32[]{:S(2)}) async-start(bf16[128,72,128]{2,1,0:T(8,128)(2,1)} %get-tuple-element.7), calls=%async_computation | async-start | bytes 4718592 | tf_op jit(solution)/shard_map/all_to_all | solution.py:239
  52.5 43.9 %copy-start.3 = (f32[256]{0:T(256)S(1)}, f32[256]{0:T(256)}, u32[]{:S(2)}) copy-start(f32[256]{0:T(256)} %param.12) | copy-start | bytes 3076
  52.5 43.9 %copy-start.1 = (f32[256,512]{1,0:T(8,128)S(1)}, f32[256,512]{1,0:T(8,128)}, u32[]{:S(2)}) copy-start(f32[256,512]{1,0:T(8,128)} %constant.29.clone) | copy-start | bytes 1572868
  85.0 1.4 %copy-start = (bf16[128,72,128]{2,1,0:T(8,128)(2,1)}, bf16[128,72,128]{2,1,0:T(8,128)(2,1)S(1)}, u32[]{:S(2)}) copy-start(bf16[128,72,128]{2,1,0:T(8,128)(2,1)S(1)} %all-to-all-done.whole_ref) | copy-start | bytes 7077892
  91.7 13.4 %all-to-all-start.2 = ((bf16[16,96,128]{2,1,0:T(8,128)(2,1)}), bf16[16,96,128]{2,1,0:T(8,128)(2,1)S(1)}, u32[]{:S(2)}, u32[]{:S(2)}) async-start(bf16[16,96,128]{2,1,0:T(8,128)(2,1)} %stack.13), calls=%async_computation.2 | async-start | bytes 786432 | tf_op jit(solution)/shard_map/all_to_all | solution.py:239
  105.1 0.7 copy-start.2

commit v2 on v1

v2 whole, which is shorter than its diff:
```python
import functools

import numpy as np
import jax
import jax.numpy as jnp
from jax import lax
from jax.experimental import pallas as pl
from jax.experimental.pallas import tpu as pltpu
from jax.sharding import PartitionSpec as P

LANES = 128
ROWS = 512
SAMPLES = 1536
CLASSES = 32
GROUP = ROWS // CLASSES
TILES = SAMPLES // LANES
N_IN = 8
N_X = 16
DEVICES = N_IN * N_X
SLOTS = 64
HALF = LANES // 2
CODES = SLOTS + SLOTS // 2
MIB = 1024 * 1024


def iota(shape, dim):
    return lax.broadcasted_iota(jnp.int32, shape, dim)


def narrow_windows(shift_ref):
    lane = iota((CLASSES, LANES), 1)
    widest = jnp.zeros((CLASSES, 1), jnp.float32)
    for k in range(TILES):
        u = (lane + shift_ref[:, k * LANES : (k + 1) * LANES]).astype(jnp.float32)
        widest = jnp.maximum(widest, jnp.max(u, axis=1, keepdims=True) - jnp.min(u, axis=1, keepdims=True))
    return jnp.max(widest) < LANES


def moveout(narrow, rows_ready, x_ref, shift_ref, weight_ref, moved_ref):
    lane = iota((8, LANES), 1)

    def lanes_of(values, index):
        return jnp.take_along_axis(values, index, axis=1, mode="promise_in_bounds")

    def first_below(u, sources):
        chosen = sources[2]
        for n in (1, 0):
            if sources[n] is not chosen:
                chosen = jnp.where(u < (n + 1) * LANES, sources[n], chosen)
        return chosen

    def one_tile(e, narrow, k, shifts, weights):
        places = lane + shifts
        lowest = jnp.min(places.astype(jnp.float32), axis=1, keepdims=True).astype(jnp.int32)
        lowest = jnp.broadcast_to(lowest, (8, LANES))
        for c in range(8):
            rows = pl.ds(pl.multiple_of(e * 8 * GROUP + c * GROUP, GROUP), GROUP)
            early = jnp.broadcast_to(places[c : c + 1], (8, LANES))
            weight = jnp.broadcast_to(weights[c : c + 1], (8, LANES))
            rest = 1.0 - weight
            blank = jnp.zeros((8, LANES), jnp.float32)
            halves = [[], []]
            for n in range(3):
                if k + n < TILES:
                    both = x_ref[rows, (k + n) * LANES : (k + n + 1) * LANES].astype(jnp.float32)
                    halves[0].append(both[:8])
                    halves[1].append(both[8:])
                else:
                    halves[0].append(blank)
                    halves[1].append(blank)
            picks = []
            if narrow:
                low = jnp.broadcast_to(lowest[c : c + 1], (8, LANES))
                for step in range(2):
                    held = low + step + ((lane - low - step) & (LANES - 1))
                    picks.append(((early + step) & (LANES - 1), held))
            parts = []
            for sources in halves:
                if narrow:
                    values = [lanes_of(first_below(held, sources), index) for index, held in picks]
                else:
                    values = []
                    for step in range(2):
                        u = early + step
                        index = u & (LANES - 1)
                        got = [s if s is blank else lanes_of(s, index) for s in sources]
                        values.append(first_below(u, got))
                parts.append(rest * values[0] + weight * values[1])
            moved_ref[rows, k * LANES : (k + 1) * LANES] = jnp.concatenate(parts, axis=0).astype(jnp.bfloat16)

    def eight_classes(narrow, e):
        tables = pl.ds(pl.multiple_of(e * 8, 8), 8)
        for k in range(TILES):
            at = slice(k * LANES, (k + 1) * LANES)
            one_tile(e, narrow, k, shift_ref[tables, at], weight_ref[tables, at])

    def step(e, carry):
        rows_ready(e)

        @pl.when(narrow)
        def _():
            eight_classes(True, e)

        @pl.when(jnp.logical_not(narrow))
        def _():
            eight_classes(False, e)

        return carry

    lax.fori_loop(0, CLASSES // 8, step, 0)


def slot_of_rows(owner_row):
    owners = owner_row.astype(jnp.float32)
    blocks = [owners[:, b * LANES : (b + 1) * LANES] for b in range(ROWS // LANES)]
    columns = [jnp.transpose(jnp.broadcast_to(b, (LANES, LANES))) for b in blocks]
    earlier = iota((LANES, LANES), 0) < iota((LANES, LANES), 1)
    ranks = []
    for b, block in enumerate(blocks):
        total = jnp.zeros((LANES, LANES), jnp.float32)
        for a in range(b + 1):
            same = columns[a] == block
            if a == b:
                same = same & earlier
            total = total + jnp.where(same, 1.0, 0.0)
        ranks.append(jnp.sum(total, axis=0, keepdims=True))
    rank = jnp.concatenate(ranks, axis=1).astype(jnp.int32)
    return (owner_row & (N_X - 1)) * SLOTS + (owner_row >> 4) * 8 + rank


def spread(slot, place_ref):
    for m in range(N_X * SLOTS // LANES):
        here = iota((LANES, ROWS), 0) + m * LANES == slot
        place_ref[m * LANES : (m + 1) * LANES, :] = jnp.where(here, 1.0, 0.0).astype(jnp.bfloat16)


def pack_kernel(
    owner_hbm, cell_hbm, shift_hbm, weight_hbm, x_hbm, out_hbm,
    owner_ref, cell_ref, shift_ref, weight_ref, x_ref, moved_ref, place_ref, out_ref, small_sem, in_sem, out_sem,
):
    quarter = ROWS // 4
    small = [
        pltpu.make_async_copy(source, target, small_sem.at[n])
        for n, (source, target) in enumerate(
            [(owner_hbm, owner_ref), (cell_hbm, cell_ref), (shift_hbm, shift_ref), (weight_hbm, weight_ref)]
        )
    ]
    for copy in small:
        copy.start()

    def arrival(e):
        rows = pl.ds(pl.multiple_of(e * quarter, quarter), quarter)
        return pltpu.make_async_copy(x_hbm.at[rows], x_ref.at[rows], in_sem.at[e])

    def departure(m):
        groups = pl.ds(2 * m, 2)
        return pltpu.make_async_copy(out_ref.at[:, groups], out_hbm.at[:, groups], out_sem.at[m])

    for e in range(4):
        arrival(e).start()
    small[0].wait()
    slot = slot_of_rows(owner_ref[...])
    spread(slot, place_ref)
    small[1].wait()
    code = ((slot >> 3) & 1) * LANES + cell_ref[...] + 1
    line = (slot >> 6) * 8 + ((slot >> 4) & 3)
    held = jnp.where(iota((LANES, ROWS), 0) == line, code.astype(jnp.float32), 0.0).astype(jnp.bfloat16)
    lanes = jnp.where((iota((LANES, ROWS), 0) & 15) == (slot & 15), 1.0, 0.0).astype(jnp.bfloat16)
    codes = lax.dot_general(
        held, lanes, (((1,), (1,)), ((), ())), preferred_element_type=jnp.float32
    ).astype(jnp.bfloat16)
    for x in range(N_X):
        for i in range(N_IN):
            out_ref[i, x, CODES : CODES + 8, :] = codes[x * 8 : (x + 1) * 8]
    small[2].wait()
    small[3].wait()
    moveout(
        narrow_windows(shift_ref), lambda e: arrival(e).wait(), x_ref, shift_ref, weight_ref, moved_ref
    )
    low = iota((SLOTS // 2, LANES), 1) < HALF

    def two_groups(m, carry):
        place = place_ref[pl.ds(pl.multiple_of(m * LANES, LANES), LANES), :]
        for n in range(N_IN // 2):
            result = jnp.dot(
                place, moved_ref[:, 3 * n * LANES : 3 * (n + 1) * LANES], preferred_element_type=jnp.float32
            )
            for x in range(2):
                block = result[x * SLOTS : (x + 1) * SLOTS]
                out_ref[2 * n, 2 * m + x, 0:SLOTS, :] = block[:, :LANES].astype(jnp.bfloat16)
                out_ref[2 * n + 1, 2 * m + x, 0:SLOTS, :] = block[:, 2 * LANES :].astype(jnp.bfloat16)
                middle = block[:, LANES : 2 * LANES]
                first, second = middle[: SLOTS // 2], middle[SLOTS // 2 :]
                even = jnp.where(low, first, pltpu.roll(second, HALF, 1))
                odd = jnp.where(low, pltpu.roll(first, HALF, 1), second)
                out_ref[2 * n, 2 * m + x, SLOTS:CODES, :] = even.astype(jnp.bfloat16)
                out_ref[2 * n + 1, 2 * m + x, SLOTS:CODES, :] = odd.astype(jnp.bfloat16)
        departure(m).start()
        return carry

    lax.fori_loop(0, N_X // 2, two_groups, 0)
    for m in range(N_X // 2):
        departure(m).wait()


def stack_kernel(slots_ref, out_hbm, select_ref, out_ref, out_sem):
    bins = (iota((2 * LANES, LANES), 0) + 1).astype(jnp.float32).astype(jnp.bfloat16)
    depth = DEVICES * 16
    ones = jnp.ones((depth, LANES), jnp.bfloat16)
    lines = []
    for j in range(DEVICES // 8):
        line = jnp.zeros((8, LANES), jnp.float32)
        for g in range(8):
            mine = (iota((8, LANES), 1) >> 4) == g
            codes = slots_ref[8 * j + g, CODES : CODES + 8, :].astype(jnp.float32)
            line = jnp.where(mine, codes, line)
        lines.append(line)
    low = iota((32, LANES), 1) < HALF

    def departure(p):
        return pltpu.make_async_copy(out_ref.at[4 * p : 4 * p + 4], out_hbm.at[4 * p : 4 * p + 4], out_sem.at[p])

    for p in range(4):
        for j in range(DEVICES // 8):
            row = jnp.broadcast_to(lines[j][p : p + 1], (16, LANES)).astype(jnp.bfloat16)
            row = jnp.concatenate([row] * 16, axis=0)
            select_ref[:, j * LANES : (j + 1) * LANES] = jnp.where(
                bins == row, jnp.bfloat16(1), jnp.bfloat16(0)
            )
        select = select_ref[...]
        full = slots_ref[:, 16 * p : 16 * p + 16, :].reshape(depth, LANES)
        q = p % 2
        half = slots_ref[:, SLOTS + 16 * q : SLOTS + 16 * q + 16, :].reshape(depth, LANES)
        sums = jnp.dot(select, jnp.concatenate([full, ones], axis=1), preferred_element_type=jnp.float32)
        fold = jnp.maximum(sums[:, LANES:], 1.0)
        mean = sums[:, :LANES] / fold
        part = jnp.dot(select, half, preferred_element_type=jnp.float32) / fold
        for x in range(4):
            rows = slice(64 * x, 64 * x + 64)
            out_ref[4 * p + x, 0:64, :] = mean[rows].astype(jnp.bfloat16)
            first, second = part[64 * x : 64 * x + 32], part[64 * x + 32 : 64 * x + 64]
            if p < 2:
                packed = jnp.where(low, first, pltpu.roll(second, HALF, 1))
            else:
                packed = jnp.where(low, pltpu.roll(first, HALF, 1), second)
            out_ref[4 * p + x, 64:96, :] = packed.astype(jnp.bfloat16)
        departure(p).start()
    for p in range(4):
        departure(p).wait()


def filter_kernel(order_ref, matrix_ref, slab_ref, out_ref):
    whole_at, shared_at = order_ref[0], order_ref[1]
    matrix = matrix_ref[...]
    count = N_X * 16

    def apply(block):
        return lax.dot_general(block, matrix, (((0,), (0,)), ((), ())), preferred_element_type=jnp.float32)

    for i in range(4):
        full = slab_ref[:, 16 * i : 16 * i + 16, :].reshape(count, LANES)
        out_ref[pl.ds(whole_at, LANES), i, :] = apply(full)
    for i in range(2):
        pair = slab_ref[:, 64 + 16 * i : 80 + 16 * i, :].reshape(count, LANES)
        both = apply(pair)
        out_ref[pl.ds(shared_at, HALF), i, :] = both[:HALF]
        out_ref[pl.ds(shared_at, HALF), i + 2, :] = both[HALF:]


def call(kernel, name, out_shape, scratch, in_specs, out_specs, mib):
    return pl.pallas_call(
        kernel,
        out_shape=out_shape,
        scratch_shapes=scratch,
        name=name,
        in_specs=in_specs,
        out_specs=out_specs,
        compiler_params=pltpu.CompilerParams(vmem_limit_bytes=mib * MIB),
    )


def crossline_filter(gains):
    count = gains.shape[0]
    index = np.arange(count)
    phase = 2.0 * np.pi * (index[:, None] * index[None, :] % count) / count
    basis = np.concatenate([np.cos(phase), np.sin(phase)], axis=1).astype(np.float32)
    scaled = basis * jnp.concatenate([gains, gains])[None, :]
    dims = (((1,), (1,)), ((), ()))
    product = lax.dot_general(scaled, jnp.asarray(basis), dims, precision=lax.Precision.HIGHEST)
    return (product / count).astype(jnp.bfloat16)


def exchange(block, axes):
    return lax.all_to_all(block, axes, split_axis=0, concat_axis=0, tiled=True)


def shards(traces, owner, cell, shift_table, weight_table, gains):
    bf16, dma = jnp.bfloat16, pltpu.SemaphoreType.DMA
    vmem, smem = pl.BlockSpec(memory_space=pltpu.VMEM), pl.BlockSpec(memory_space=pltpu.SMEM)
    hbm = pl.BlockSpec(memory_space=pltpu.HBM)
    owner_row, cell_row = owner.reshape(1, ROWS), cell.reshape(1, ROWS)
    out = (N_IN, N_X, CODES + 8, LANES)
    slots = call(
        pack_kernel,
        "pack",
        jax.ShapeDtypeStruct(out, bf16),
        [
            pltpu.VMEM((1, ROWS), jnp.int32),
            pltpu.VMEM((1, ROWS), jnp.int32),
            pltpu.VMEM((CLASSES, SAMPLES), jnp.int32),
            pltpu.VMEM((CLASSES, SAMPLES), jnp.float32),
            pltpu.VMEM((ROWS, SAMPLES), bf16),
            pltpu.VMEM((ROWS, SAMPLES), bf16),
            pltpu.VMEM((N_X * SLOTS, ROWS), bf16),
            pltpu.VMEM(out, bf16),
            dma((4,)),
            dma((4,)),
            dma((N_X // 2,)),
        ],
        [hbm] * 5,
        hbm,
        60,
    )(owner_row, cell_row, shift_table, weight_table, traces)
    slots = exchange(slots.reshape(DEVICES, CODES + 8, LANES), ("inline", "xline"))
    matrix = crossline_filter(gains)
    stacked = call(
        stack_kernel,
        "stack",
        jax.ShapeDtypeStruct((N_X, 96, LANES), bf16),
        [pltpu.VMEM((2 * LANES, DEVICES * 16), bf16), pltpu.VMEM((N_X, 96, LANES), bf16), dma((4,))],
        [vmem],
        hbm,
        32,
    )(slots)
    slab = exchange(stacked, "xline")
    odd = lax.axis_index("inline") % 2
    order = jnp.stack([odd * HALF, (1 - odd) * LANES])
    return call(
        filter_kernel,
        "crossline",
        jax.ShapeDtypeStruct((SAMPLES // N_IN, 4, N_X * 16), jnp.float32),
        [],
        [smem, vmem, vmem],
        vmem,
        16,
    )(order, matrix, slab)


def solution(mesh):
    split = P(("inline", "xline"))
    placed = (P(("inline", "xline"), None), P(("inline", "xline"), None), split, P(), P(), P())
    return jax.shard_map(
        shards, mesh=mesh, in_specs=placed, out_specs=P("inline", "xline", None), check_vma=False
    )
```

time: 109 us -> 87.6 us (0.80)
  blocking collectives: 30.3 us -> 0 us
  waiting for transfers between devices: 39.9 us -> 50.6 us
  starting transfers between devices: 8.66 us -> 15.9 us
  Pallas kernels: 25.2 us -> 18 us
  local copies, waits for them, and re-layouts: 2.17 us -> 0.75 us
    all_to_all x1 -> x0, blocking collectives: 30.3 us -> none  [exchange(): return lax.all_to_all(block, axes, split_axis=0, concat_axis=0, tiled=True)]
    all_to_all x2, waiting for transfers between devices: 39.9 us -> 50.6 us  [exchange(): return lax.all_to_all(block, axes, split_axis=0, concat_axis=0, tiled=True)]
    all_to_all x2, starting transfers between devices: 8.66 us -> 15.9 us  [exchange(): return lax.all_to_all(block, axes, split_axis=0, concat_axis=0, tiled=True)]
    pallas_call x2 -> x1, Pallas kernels: 17.5 us -> 12.5 us  [shards(): call(pack_kernel, 'pack', jax.ShapeDtypeStruct(out, bf16), [pltpu.VMEM((1...]
    pallas_call x1, Pallas kernels: 5.29 us -> 3.61 us  [shards(): call(stack_kernel, 'stack', jax.ShapeDtypeStruct((N_X, 96, LANES), bf16),...]
    unnamed x8 -> x4, local copies, waits for them, and re-layouts: 2.17 us -> 0.75 us
where the time goes in v2:
time: 87.6 us; the launch traced here: 87.3 us
  waiting for transfers between devices  50.6 us (58%)
  Pallas kernels  18 us (21%)
  starting transfers between devices  15.9 us (18%)
  matrix products  1.82 us (2%)
    all_to_all x2, waiting for transfers between devices, exchange(): return lax.all_to_all(block, axes, split_axis=0, concat_axis=0, tiled=True)  50.6 us
    all_to_all x2, starting transfers between devices, exchange(): return lax.all_to_all(block, axes, split_axis=0, concat_axis=0, tiled=True)  15.9 us
    pallas_call x1, Pallas kernels, shards(): call(pack_kernel, 'pack', jax.ShapeDtypeStruct(out, bf16), [pltpu.VMEM((1...  12.5 us
    pallas_call x1, Pallas kernels, shards(): call(stack_kernel, 'stack', jax.ShapeDtypeStruct((N_X, 96, LANES), bf16),...  3.61 us
    pallas_call x1, Pallas kernels, shards(): call(filter_kernel, 'crossline', jax.ShapeDtypeStruct((SAMPLES // N_IN, 4...  1.87 us
    dot_general x1, matrix products, crossline_filter(): lax.dot_general(scaled, jnp.asarray(basis), dims, precision=lax.Precision...  1.82 us
  transfers between devices with their start and end apart: 2, of which 2 were waited for; matrix products, arithmetic and copies ran while one was open for 2% of the time, Pallas kernels for 0%

profile of v2, /device:TPU:0, one launch (start us, length us, event | category | flops | bytes accessed | tf_op | source)
XLA Modules:
  0.0 87.3 jit_solution(3539281336385522199)
XLA Ops:
  0.0 12.5 %pack.1 = bf16[8,16,104,128]{3,2,1,0:T(8,128)(2,1)} custom-call(s32[1,512]{1,0:T(1,128)} %bitcast.7, s32[1,512]{1,0:T(1,128)} %bitcast.8, s32[32,1536]{1,0:T(8,128)} %shift_hbm.1, f32[32,1536]{1,0:T(8,128)} %weight_hbm.1, bf16[512,1536]{1,0:T(8,128)(2,1)} %x_hbm.1), custom_call_target="tpu_custom_call" | custom-call | tf_op jit(solution)/shard_map/pack/pallas_call | solution.py:303
  12.5 11.1 %all-to-all-start = ((bf16[128,104,128]{2,1,0:T(8,128)(2,1)}), bf16[128,104,128]{2,1,0:T(8,128)(2,1)S(1)}, u32[]{:S(2)}, u32[]{:S(2)}) async-start(bf16[128,104,128]{2,1,0:T(8,128)(2,1)} %bitcast.6), calls=%async_computation | async-start | bytes 6815744 | tf_op jit(solution)/shard_map/all_to_all | solution.py:294
  23.7 0.0 copy-start.1
  23.7 43.1 %all-to-all-done.slots_ref = bf16[128,104,128]{2,1,0:T(8,128)(2,1)S(1)} async-done(((bf16[128,104,128]{2,1,0:T(8,128)(2,1)}), bf16[128,104,128]{2,1,0:T(8,128)(2,1)S(1)}, u32[]{:S(2)}, u32[]{:S(2)}) %all-to-all-start) | async-done | bytes 3407904 | tf_op jit(solution)/shard_map/all_to_all | solution.py:294
  66.8 3.6 %stack.13 = bf16[16,96,128]{2,1,0:T(8,128)(2,1)S(1)} custom-call(bf16[128,104,128]{2,1,0:T(8,128)(2,1)S(1)} %all-to-all-done.slots_ref), custom_call_target="tpu_custom_call" | custom-call | tf_op jit(solution)/shard_map/stack/pallas_call | solution.py:326
  70.4 0.0 copy-start
  70.5 0.7 copy-done
  71.2 4.8 %all-to-all-start.1 = ((bf16[16,96,128]{2,1,0:T(8,128)(2,1)}), bf16[16,96,128]{2,1,0:T(8,128)(2,1)S(1)}, u32[]{:S(2)}, u32[]{:S(2)}) async-start(bf16[16,96,128]{2,1,0:T(8,128)(2,1)} %copy-done), calls=%async_computation.1 | async-start | bytes 786432 | tf_op jit(solution)/shard_map/all_to_all | solution.py:294
  76.0 0.1 pad_add_fusion.order_ref
  76.0 0.0 copy-done.1
  76.1 1.8 %fusion.matrix_ref = bf16[256,256]{1,0:T(8,128)(2,1)S(1)} fusion(f32[256,512]{1,0:T(8,128)} %constant.29.clone, f32[512]{0:T(512)S(1)} %pad_maximum_fusion), kind=kOutput, calls=%fused_computation.1 | convolution fusion | flops 402915328 | bytes 657408 | tf_op jit(solution)/shard_map/dot_general | solution.py:289
  77.9 7.5 %all-to-all-done.1.slab_ref = bf16[16,96,128]{2,1,0:T(8,128)(2,1)S(1)} async-done(((bf16[16,96,128]{2,1,0:T(8,128)(2,1)}), bf16[16,96,128]{2,1,0:T(8,128)(2,1)S(1)}, u32[]{:S(2)}, u32[]{:S(2)}) %all-to-all-start.1) | async-done | bytes 393248 | tf_op jit(solution)/shard_map/all_to_all | solution.py:294
  85.4 1.9 %crossline.1 = f32[192,4,256]{2,1,0:T(4,128)} custom-call(s32[2]{0:T(128)S(1)} %pad_add_fusion.order_ref, bf16[256,256]{1,0:T(8,128)(2,1)S(1)} %fusion.matrix_ref, bf16[16,96,128]{2,1,0:T(8,128)(2,1)S(1)} %all-to-all-done.1.slab_ref), custom_call_target="tpu_custom_call" | custom-call | tf_op jit(solution)/shard_map/crossline/pallas_call | solution.py:338
  (1 shorter events, 0.0 us)
Async XLA Ops:
  12.5 54.3 %all-to-all-start = ((bf16[128,104,128]{2,1,0:T(8,128)(2,1)}), bf16[128,104,128]{2,1,0:T(8,128)(2,1)S(1)}, u32[]{:S(2)}, u32[]{:S(2)}) async-start(bf16[128,104,128]{2,1,0:T(8,128)(2,1)} %bitcast.6), calls=%async_computation | async-start | bytes 6815744 | tf_op jit(solution)/shard_map/all_to_all | solution.py:294
  23.7 52.4 %copy-start.1 = (f32[256]{0:T(256)S(1)}, f32[256]{0:T(256)}, u32[]{:S(2)}) copy-start(f32[256]{0:T(256)} %param.12) | copy-start | bytes 3076
  70.4 0.7 copy-start
  71.2 14.2 %all-to-all-start.1 = ((bf16[16,96,128]{2,1,0:T(8,128)(2,1)}), bf16[16,96,128]{2,1,0:T(8,128)(2,1)S(1)}, u32[]{:S(2)}, u32[]{:S(2)}) async-start(bf16[16,96,128]{2,1,0:T(8,128)(2,1)} %copy-done), calls=%async_computation.1 | async-start | bytes 786432 | tf_op jit(solution)/shard_map/all_to_all | solution.py:294

commit v3 on v2

--- a/solution.py
+++ b/solution.py
@@ -27,87 +27,61 @@
     return lax.broadcasted_iota(jnp.int32, shape, dim)
 
 
-def narrow_windows(shift_ref):
-    lane = iota((CLASSES, LANES), 1)
-    widest = jnp.zeros((CLASSES, 1), jnp.float32)
-    for k in range(TILES):
-        u = (lane + shift_ref[:, k * LANES : (k + 1) * LANES]).astype(jnp.float32)
-        widest = jnp.maximum(widest, jnp.max(u, axis=1, keepdims=True) - jnp.min(u, axis=1, keepdims=True))
-    return jnp.max(widest) < LANES
-
-
-def moveout(narrow, rows_ready, x_ref, shift_ref, weight_ref, moved_ref):
+def table_places(shift_ref, places_ref):
     lane = iota((8, LANES), 1)
-
-    def lanes_of(values, index):
-        return jnp.take_along_axis(values, index, axis=1, mode="promise_in_bounds")
-
-    def first_below(u, sources):
-        chosen = sources[2]
-        for n in (1, 0):
-            if sources[n] is not chosen:
-                chosen = jnp.where(u < (n + 1) * LANES, sources[n], chosen)
-        return chosen
-
-    def one_tile(e, narrow, k, shifts, weights):
-        places = lane + shifts
-        lowest = jnp.min(places.astype(jnp.float32), axis=1, keepdims=True).astype(jnp.int32)
-        lowest = jnp.broadcast_to(lowest, (8, LANES))
-        for c in range(8):
-            rows = pl.ds(pl.multiple_of(e * 8 * GROUP + c * GROUP, GROUP), GROUP)
-            early = jnp.broadcast_to(places[c : c + 1], (8, LANES))
-            weight = jnp.broadcast_to(weights[c : c + 1], (8, LANES))
-            rest = 1.0 - weight
-            blank = jnp.zeros((8, LANES), jnp.float32)
-            halves = [[], []]
-            for n in range(3):
-                if k + n < TILES:
-                    both = x_ref[rows, (k + n) * LANES : (k + n + 1) * LANES].astype(jnp.float32)
-                    halves[0].append(both[:8])
-                    halves[1].append(both[8:])
-                else:
-                    halves[0].append(blank)
-                    halves[1].append(blank)
-            picks = []
-            if narrow:
-                low = jnp.broadcast_to(lowest[c : c + 1], (8, LANES))
-                for step in range(2):
-                    held = low + step + ((lane - low - step) & (LANES - 1))
-                    picks.append(((early + step) & (LANES - 1), held))
-            parts = []
-            for sources in halves:
-                if narrow:
-                    values = [lanes_of(first_below(held, sources), index) for index, held in picks]
-                else:
-                    values = []
-                    for step in range(2):
-                        u = early + step
-                        index = u & (LANES - 1)
-                        got = [s if s is blank else lanes_of(s, index) for s in sources]
-                        values.append(first_below(u, got))
-                parts.append(rest * values[0] + weight * values[1])
-            moved_ref[rows, k * LANES : (k + 1) * LANES] = jnp.concatenate(parts, axis=0).astype(jnp.bfloat16)
-
-    def eight_classes(narrow, e):
-        tables = pl.ds(pl.multiple_of(e * 8, 8), 8)
+    widest = jnp.zeros((8, 1), jnp.float32)
+    for e in range(CLASSES // 8):
+        rows = slice(8 * e, 8 * e + 8)
         for k in range(TILES):
             at = slice(k * LANES, (k + 1) * LANES)
-            one_tile(e, narrow, k, shift_ref[tables, at], weight_ref[tables, at])
-
-    def step(e, carry):
-        rows_ready(e)
-
-        @pl.when(narrow)
-        def _():
-            eight_classes(True, e)
-
-        @pl.when(jnp.logical_not(narrow))
-        def _():
-            eight_classes(False, e)
-
-        return carry
-
-    lax.fori_loop(0, CLASSES // 8, step, 0)
+            u = lane + shift_ref[rows, at]
+            low = jnp.min(u.astype(jnp.float32), axis=1, keepdims=True)
+            high = jnp.max(u.astype(jnp.float32), axis=1, keepdims=True)
+            widest = jnp.maximum(widest, high - low)
+            low = jnp.broadcast_to(low.astype(jnp.int32), (8, LANES))
+            for step in range(2):
+                places_ref[step, rows, at] = (u + step) & (LANES - 1)
+                places_ref[2 + step, rows, at] = low + step + ((lane - low - step) & (LANES - 1))
+    return jnp.max(widest) < LANES
+
+
+def lanes_of(values, index):
+    return jnp.take_along_axis(values, index, axis=1, mode="promise_in_bounds")
+
+
+def first_below(u, sources):
+    chosen = sources[2]
+    for n in (1, 0):
+        if sources[n] is not chosen:
+            chosen = jnp.where(u < (n + 1) * LANES, sources[n], chosen)
+    return chosen
+
+
+def moveout(narrow, k, c, row_of, rows, x_ref, shift_ref, weight_ref, places_ref, moved_ref):
+    at = slice(k * LANES, (k + 1) * LANES)
+    weight = row_of(weight_ref, c, at)
+    rest = 1.0 - weight
+    blank = jnp.zeros((8, LANES), jnp.float32)
+    halves = [[], []]
+    for n in range(3):
+        both = None
+        if k + n < TILES:
+            both = x_ref[rows, (k + n) * LANES : (k + n + 1) * LANES].astype(jnp.float32)
+        halves[0].append(blank if both is None else both[:8])
+        halves[1].append(blank if both is None else both[8:])
+    parts = [[], []]
+    for step in range(2):
+        if narrow:
+            index, held = row_of(places_ref.at[step], c, at), row_of(places_ref.at[2 + step], c, at)
+            for h, sources in enumerate(halves):
+                parts[h].append(lanes_of(first_below(held, sources), index))
+        else:
+            u = iota((8, LANES), 1) + row_of(shift_ref, c, at) + step
+            for h, sources in enumerate(halves):
+                got = [s if s is blank else lanes_of(s, u & (LANES - 1)) for s in sources]
+                parts[h].append(first_below(u, got))
+    mixed = [rest * first + weight * second for first, second in parts]
+    moved_ref[rows, at] = jnp.concatenate(mixed, axis=0).astype(jnp.bfloat16)
 
 
 def slot_of_rows(owner_row):
@@ -136,32 +110,19 @@
 
 def pack_kernel(
     owner_hbm, cell_hbm, shift_hbm, weight_hbm, x_hbm, out_hbm,
-    owner_ref, cell_ref, shift_ref, weight_ref, x_ref, moved_ref, place_ref, out_ref, small_sem, in_sem, out_sem,
+    owner_ref, cell_ref, shift_ref, weight_ref, x_ref, places_ref, moved_ref, place_ref, out_ref, in_sem, out_sem,
 ):
-    quarter = ROWS // 4
-    small = [
-        pltpu.make_async_copy(source, target, small_sem.at[n])
-        for n, (source, target) in enumerate(
-            [(owner_hbm, owner_ref), (cell_hbm, cell_ref), (shift_hbm, shift_ref), (weight_hbm, weight_ref)]
-        )
+    arrays = [
+        (owner_hbm, owner_ref), (cell_hbm, cell_ref), (shift_hbm, shift_ref), (weight_hbm, weight_ref), (x_hbm, x_ref),
     ]
-    for copy in small:
+    arrivals = [pltpu.make_async_copy(a, b, in_sem.at[n]) for n, (a, b) in enumerate(arrays)]
+    departures = [pltpu.make_async_copy(out_ref.at[i], out_hbm.at[i], out_sem.at[i]) for i in range(N_IN)]
+    for copy in arrivals:
         copy.start()
-
-    def arrival(e):
-        rows = pl.ds(pl.multiple_of(e * quarter, quarter), quarter)
-        return pltpu.make_async_copy(x_hbm.at[rows], x_ref.at[rows], in_sem.at[e])
-
-    def departure(m):
-        groups = pl.ds(2 * m, 2)
-        return pltpu.make_async_copy(out_ref.at[:, groups], out_hbm.at[:, groups], out_sem.at[m])
-
-    for e in range(4):
-        arrival(e).start()
-    small[0].wait()
+    arrivals[0].wait()
     slot = slot_of_rows(owner_ref[...])
     spread(slot, place_ref)
-    small[1].wait()
+    arrivals[1].wait()
     code = ((slot >> 3) & 1) * LANES + cell_ref[...] + 1
     line = (slot >> 6) * 8 + ((slot >> 4) & 3)
     held = jnp.where(iota((LANES, ROWS), 0) == line, code.astype(jnp.float32), 0.0).astype(jnp.bfloat16)
@@ -172,35 +133,69 @@
     for x in range(N_X):
         for i in range(N_IN):
             out_ref[i, x, CODES : CODES + 8, :] = codes[x * 8 : (x + 1) * 8]
-    small[2].wait()
-    small[3].wait()
-    moveout(
-        narrow_windows(shift_ref), lambda e: arrival(e).wait(), x_ref, shift_ref, weight_ref, moved_ref
-    )
+    for copy in arrivals[2:]:
+        copy.wait()
     low = iota((SLOTS // 2, LANES), 1) < HALF
 
-    def two_groups(m, carry):
-        place = place_ref[pl.ds(pl.multiple_of(m * LANES, LANES), LANES), :]
-        for n in range(N_IN // 2):
-            result = jnp.dot(
-                place, moved_ref[:, 3 * n * LANES : 3 * (n + 1) * LANES], preferred_element_type=jnp.float32
-            )
-            for x in range(2):
-                block = result[x * SLOTS : (x + 1) * SLOTS]
-                out_ref[2 * n, 2 * m + x, 0:SLOTS, :] = block[:, :LANES].astype(jnp.bfloat16)
-                out_ref[2 * n + 1, 2 * m + x, 0:SLOTS, :] = block[:, 2 * LANES :].astype(jnp.bfloat16)
-                middle = block[:, LANES : 2 * LANES]
-                first, second = middle[: SLOTS // 2], middle[SLOTS // 2 :]
-                even = jnp.where(low, first, pltpu.roll(second, HALF, 1))
-                odd = jnp.where(low, pltpu.roll(first, HALF, 1), second)
-                out_ref[2 * n, 2 * m + x, SLOTS:CODES, :] = even.astype(jnp.bfloat16)
-                out_ref[2 * n + 1, 2 * m + x, SLOTS:CODES, :] = odd.astype(jnp.bfloat16)
-        departure(m).start()
-        return carry
-
-    lax.fori_loop(0, N_X // 2, two_groups, 0)
-    for m in range(N_X // 2):
-        departure(m).wait()
+    def place_pair(n):
+        result = jnp.dot(
+            place_ref[...], moved_ref[:, 2 * n * LANES : 2 * (n + 1) * LANES], preferred_element_type=jnp.float32
+        )
+        for k in (2 * n, 2 * n + 1):
+            even = 2 * (k // 3)
+            for x in range(N_X):
+                block = result[x * SLOTS : (x + 1) * SLOTS, (k - 2 * n) * LANES : (k - 2 * n + 1) * LANES]
+                if k % 3 != 1:
+                    out_ref[even + k % 3 // 2, x, 0:SLOTS, :] = block.astype(jnp.bfloat16)
+                    continue
+                first, second = block[: SLOTS // 2], block[SLOTS // 2 :]
+                out_ref[even, x, SLOTS:CODES, :] = jnp.where(
+                    low, first, pltpu.roll(second, HALF, 1)
+                ).astype(jnp.bfloat16)
+                out_ref[even + 1, x, SLOTS:CODES, :] = jnp.where(
+                    low, pltpu.roll(first, HALF, 1), second
+                ).astype(jnp.bfloat16)
+            if k % 3:
+                departures[even + k % 3 - 1].start()
+
+    def all_tiles(narrow):
+        refs = x_ref, shift_ref, weight_ref, places_ref, moved_ref
+
+        if narrow:
+            for n in range(TILES // 2 + 1):
+                if n < TILES // 2:
+                    for k in (2 * n, 2 * n + 1):
+                        for c in range(CLASSES):
+                            moveout(
+                                True, k, c,
+                                lambda ref, c, at: jnp.broadcast_to(ref[c : c + 1, at], (8, LANES)),
+                                slice(c * GROUP, (c + 1) * GROUP), *refs,
+                            )
+                if n:
+                    place_pair(n - 1)
+            return
+
+        def step(e, carry):
+            tables = pl.ds(pl.multiple_of(e * 8, 8), 8)
+            for c in range(8):
+                rows = pl.ds(pl.multiple_of(e * 8 * GROUP + c * GROUP, GROUP), GROUP)
+                for k in range(TILES):
+                    moveout(
+                        False, k, c,
+                        lambda ref, c, at: jnp.broadcast_to(ref[tables, at][c : c + 1], (8, LANES)),
+                        rows, *refs,
+                    )
+            return carry
+
+        lax.fori_loop(0, CLASSES // 8, step, 0)
+        for n in range(TILES // 2):
+            place_pair(n)
+
+    narrow = table_places(shift_ref, places_ref)
+    pl.when(narrow)(lambda: all_tiles(True))
+    pl.when(jnp.logical_not(narrow))(lambda: all_tiles(False))
+    for copy in departures:
+        copy.wait()
 
 
 def stack_kernel(slots_ref, out_hbm, select_ref, out_ref, out_sem):
@@ -310,12 +305,12 @@
             pltpu.VMEM((CLASSES, SAMPLES), jnp.int32),
             pltpu.VMEM((CLASSES, SAMPLES), jnp.float32),
             pltpu.VMEM((ROWS, SAMPLES), bf16),
+            pltpu.VMEM((4, CLASSES, SAMPLES), jnp.int32),
             pltpu.VMEM((ROWS, SAMPLES), bf16),
             pltpu.VMEM((N_X * SLOTS, ROWS), bf16),
             pltpu.VMEM(out, bf16),
-            dma((4,)),
-            dma((4,)),
-            dma((N_X // 2,)),
+            dma((5,)),
+            dma((N_IN,)),
         ],
         [hbm] * 5,
         hbm,

time: 87.6 us -> 81.4 us (0.929)
  Pallas kernels: 18 us -> 11.8 us
    pallas_call x1, Pallas kernels: 12.5 us -> 6.32 us  [shards(): call(pack_kernel, 'pack', jax.ShapeDtypeStruct(out, bf16), [pltpu.VMEM((1...]
where the time goes in v3:
time: 81.4 us; the launch traced here: 81.1 us
  waiting for transfers between devices  50.6 us (62%)
  starting transfers between devices  15.9 us (20%)
  Pallas kernels  11.8 us (14%)
  matrix products  1.82 us (2%)
    all_to_all x2, waiting for transfers between devices, exchange(): return lax.all_to_all(block, axes, split_axis=0, concat_axis=0, tiled=True)  50.6 us
    all_to_all x2, starting transfers between devices, exchange(): return lax.all_to_all(block, axes, split_axis=0, concat_axis=0, tiled=True)  15.9 us
    pallas_call x1, Pallas kernels, shards(): call(pack_kernel, 'pack', jax.ShapeDtypeStruct(out, bf16), [pltpu.VMEM((1...  6.32 us
    pallas_call x1, Pallas kernels, shards(): call(stack_kernel, 'stack', jax.ShapeDtypeStruct((N_X, 96, LANES), bf16),...  3.61 us
    pallas_call x1, Pallas kernels, shards(): call(filter_kernel, 'crossline', jax.ShapeDtypeStruct((SAMPLES // N_IN, 4...  1.87 us
    dot_general x1, matrix products, crossline_filter(): lax.dot_general(scaled, jnp.asarray(basis), dims, precision=lax.Precision...  1.82 us
  transfers between devices with their start and end apart: 2, of which 2 were waited for; matrix products, arithmetic and copies ran while one was open for 2% of the time, Pallas kernels for 0%

profile of v3, /device:TPU:0, one launch (start us, length us, event | category | flops | bytes accessed | tf_op | source)
XLA Modules:
  0.0 81.1 jit_solution(1062717933623408783)
XLA Ops:
  0.0 6.3 %pack.1 = bf16[8,16,104,128]{3,2,1,0:T(8,128)(2,1)} custom-call(s32[1,512]{1,0:T(1,128)} %bitcast.7, s32[1,512]{1,0:T(1,128)} %bitcast.8, s32[32,1536]{1,0:T(8,128)} %shift_hbm.1, f32[32,1536]{1,0:T(8,128)} %weight_hbm.1, bf16[512,1536]{1,0:T(8,128)(2,1)} %x_hbm.1), custom_call_target="tpu_custom_call" | custom-call | tf_op jit(solution)/shard_map/pack/pallas_call | solution.py:298
  6.3 11.1 %all-to-all-start = ((bf16[128,104,128]{2,1,0:T(8,128)(2,1)}), bf16[128,104,128]{2,1,0:T(8,128)(2,1)S(1)}, u32[]{:S(2)}, u32[]{:S(2)}) async-start(bf16[128,104,128]{2,1,0:T(8,128)(2,1)} %bitcast.6), calls=%async_computation | async-start | bytes 6815744 | tf_op jit(solution)/shard_map/all_to_all | solution.py:289
  17.5 0.0 copy-start.1
  17.5 43.1 %all-to-all-done.slots_ref = bf16[128,104,128]{2,1,0:T(8,128)(2,1)S(1)} async-done(((bf16[128,104,128]{2,1,0:T(8,128)(2,1)}), bf16[128,104,128]{2,1,0:T(8,128)(2,1)S(1)}, u32[]{:S(2)}, u32[]{:S(2)}) %all-to-all-start) | async-done | bytes 3407904 | tf_op jit(solution)/shard_map/all_to_all | solution.py:289
  60.6 3.6 %stack.13 = bf16[16,96,128]{2,1,0:T(8,128)(2,1)S(1)} custom-call(bf16[128,104,128]{2,1,0:T(8,128)(2,1)S(1)} %all-to-all-done.slots_ref), custom_call_target="tpu_custom_call" | custom-call | tf_op jit(solution)/shard_map/stack/pallas_call | solution.py:321
  64.2 0.0 copy-start
  64.2 0.7 copy-done
  65.0 4.8 %all-to-all-start.1 = ((bf16[16,96,128]{2,1,0:T(8,128)(2,1)}), bf16[16,96,128]{2,1,0:T(8,128)(2,1)S(1)}, u32[]{:S(2)}, u32[]{:S(2)}) async-start(bf16[16,96,128]{2,1,0:T(8,128)(2,1)} %copy-done), calls=%async_computation.1 | async-start | bytes 786432 | tf_op jit(solution)/shard_map/all_to_all | solution.py:289
  69.8 0.1 pad_add_fusion.order_ref
  69.8 0.0 copy-done.1
  69.9 1.8 %fusion.matrix_ref = bf16[256,256]{1,0:T(8,128)(2,1)S(1)} fusion(f32[256,512]{1,0:T(8,128)} %constant.29.clone, f32[512]{0:T(512)S(1)} %pad_maximum_fusion), kind=kOutput, calls=%fused_computation.1 | convolution fusion | flops 402915328 | bytes 657408 | tf_op jit(solution)/shard_map/dot_general | solution.py:284
  71.7 7.5 %all-to-all-done.1.slab_ref = bf16[16,96,128]{2,1,0:T(8,128)(2,1)S(1)} async-done(((bf16[16,96,128]{2,1,0:T(8,128)(2,1)}), bf16[16,96,128]{2,1,0:T(8,128)(2,1)S(1)}, u32[]{:S(2)}, u32[]{:S(2)}) %all-to-all-start.1) | async-done | bytes 393248 | tf_op jit(solution)/shard_map/all_to_all | solution.py:289
  79.2 1.9 %crossline.1 = f32[192,4,256]{2,1,0:T(4,128)} custom-call(s32[2]{0:T(128)S(1)} %pad_add_fusion.order_ref, bf16[256,256]{1,0:T(8,128)(2,1)S(1)} %fusion.matrix_ref, bf16[16,96,128]{2,1,0:T(8,128)(2,1)S(1)} %all-to-all-done.1.slab_ref), custom_call_target="tpu_custom_call" | custom-call | tf_op jit(solution)/shard_map/crossline/pallas_call | solution.py:333
  (1 shorter events, 0.0 us)
Async XLA Ops:
  6.3 54.3 %all-to-all-start = ((bf16[128,104,128]{2,1,0:T(8,128)(2,1)}), bf16[128,104,128]{2,1,0:T(8,128)(2,1)S(1)}, u32[]{:S(2)}, u32[]{:S(2)}) async-start(bf16[128,104,128]{2,1,0:T(8,128)(2,1)} %bitcast.6), calls=%async_computation | async-start | bytes 6815744 | tf_op jit(solution)/shard_map/all_to_all | solution.py:289
  17.5 52.4 %copy-start.1 = (f32[256]{0:T(256)S(1)}, f32[256]{0:T(256)}, u32[]{:S(2)}) copy-start(f32[256]{0:T(256)} %param.12) | copy-start | bytes 3076
  64.2 0.7 copy-start
  65.0 14.2 %all-to-all-start.1 = ((bf16[16,96,128]{2,1,0:T(8,128)(2,1)}), bf16[16,96,128]{2,1,0:T(8,128)(2,1)S(1)}, u32[]{:S(2)}, u32[]{:S(2)}) async-start(bf16[16,96,128]{2,1,0:T(8,128)(2,1)} %copy-done), calls=%async_computation.1 | async-start | bytes 786432 | tf_op jit(solution)/shard_map/all_to_all | solution.py:289

commit v4 on v3

--- a/solution.py
+++ b/solution.py
@@ -108,15 +108,34 @@
         place_ref[m * LANES : (m + 1) * LANES, :] = jnp.where(here, 1.0, 0.0).astype(jnp.bfloat16)
 
 
+def filter_basis():
+    count = N_X * 16
+    index = np.arange(count)
+    phase = 2.0 * np.pi * (index[:, None] * index[None, :] % count) / count
+    return np.concatenate([np.cos(phase), np.sin(phase)], axis=1).astype(np.float32)
+
+
+def crossline_filter(gains, basis):
+    count = basis.shape[0]
+    scaled = basis * jnp.concatenate([gains, gains], axis=1)
+    dims = (((1,), (1,)), ((), ()))
+    product = lax.dot_general(
+        scaled, basis, dims, precision=lax.Precision.HIGHEST, preferred_element_type=jnp.float32
+    )
+    return (product / count).astype(jnp.bfloat16)
+
+
 def pack_kernel(
-    owner_hbm, cell_hbm, shift_hbm, weight_hbm, x_hbm, out_hbm,
-    owner_ref, cell_ref, shift_ref, weight_ref, x_ref, places_ref, moved_ref, place_ref, out_ref, in_sem, out_sem,
+    owner_hbm, cell_hbm, gains_hbm, basis_hbm, shift_hbm, weight_hbm, x_hbm, out_hbm, matrix_hbm,
+    owner_ref, cell_ref, gains_ref, basis_ref, shift_ref, weight_ref, x_ref, matrix_ref, places_ref, moved_ref, place_ref, out_ref, in_sem, out_sem,
 ):
     arrays = [
         (owner_hbm, owner_ref), (cell_hbm, cell_ref), (shift_hbm, shift_ref), (weight_hbm, weight_ref), (x_hbm, x_ref),
+        (gains_hbm, gains_ref), (basis_hbm, basis_ref),
     ]
     arrivals = [pltpu.make_async_copy(a, b, in_sem.at[n]) for n, (a, b) in enumerate(arrays)]
     departures = [pltpu.make_async_copy(out_ref.at[i], out_hbm.at[i], out_sem.at[i]) for i in range(N_IN)]
+    departures.append(pltpu.make_async_copy(matrix_ref, matrix_hbm, out_sem.at[N_IN]))
     for copy in arrivals:
         copy.start()
     arrivals[0].wait()
@@ -135,6 +154,8 @@
             out_ref[i, x, CODES : CODES + 8, :] = codes[x * 8 : (x + 1) * 8]
     for copy in arrivals[2:]:
         copy.wait()
+    matrix_ref[...] = crossline_filter(gains_ref[...], basis_ref[...])
+    departures[N_IN].start()
     low = iota((SLOTS // 2, LANES), 1) < HALF
 
     def place_pair(n):
@@ -244,8 +265,9 @@
         departure(p).wait()
 
 
-def filter_kernel(order_ref, matrix_ref, slab_ref, out_ref):
-    whole_at, shared_at = order_ref[0], order_ref[1]
+def filter_kernel(matrix_ref, slab_ref, out_ref):
+    odd = lax.axis_index("inline") & 1
+    whole_at, shared_at = odd * HALF, (1 - odd) * LANES
     matrix = matrix_ref[...]
     count = N_X * 16
 
@@ -274,50 +296,42 @@
     )
 
 
-def crossline_filter(gains):
-    count = gains.shape[0]
-    index = np.arange(count)
-    phase = 2.0 * np.pi * (index[:, None] * index[None, :] % count) / count
-    basis = np.concatenate([np.cos(phase), np.sin(phase)], axis=1).astype(np.float32)
-    scaled = basis * jnp.concatenate([gains, gains])[None, :]
-    dims = (((1,), (1,)), ((), ()))
-    product = lax.dot_general(scaled, jnp.asarray(basis), dims, precision=lax.Precision.HIGHEST)
-    return (product / count).astype(jnp.bfloat16)
-
-
 def exchange(block, axes):
     return lax.all_to_all(block, axes, split_axis=0, concat_axis=0, tiled=True)
 
 
 def shards(traces, owner, cell, shift_table, weight_table, gains):
     bf16, dma = jnp.bfloat16, pltpu.SemaphoreType.DMA
-    vmem, smem = pl.BlockSpec(memory_space=pltpu.VMEM), pl.BlockSpec(memory_space=pltpu.SMEM)
+    vmem = pl.BlockSpec(memory_space=pltpu.VMEM)
     hbm = pl.BlockSpec(memory_space=pltpu.HBM)
     owner_row, cell_row = owner.reshape(1, ROWS), cell.reshape(1, ROWS)
     out = (N_IN, N_X, CODES + 8, LANES)
-    slots = call(
+    count = N_X * 16
+    slots, matrix = call(
         pack_kernel,
         "pack",
-        jax.ShapeDtypeStruct(out, bf16),
+        (jax.ShapeDtypeStruct(out, bf16), jax.ShapeDtypeStruct((count, count), bf16)),
         [
             pltpu.VMEM((1, ROWS), jnp.int32),
             pltpu.VMEM((1, ROWS), jnp.int32),
+            pltpu.VMEM((1, count), jnp.float32),
+            pltpu.VMEM((count, 2 * count), jnp.float32),
             pltpu.VMEM((CLASSES, SAMPLES), jnp.int32),
             pltpu.VMEM((CLASSES, SAMPLES), jnp.float32),
             pltpu.VMEM((ROWS, SAMPLES), bf16),
+            pltpu.VMEM((count, count), bf16),
             pltpu.VMEM((4, CLASSES, SAMPLES), jnp.int32),
             pltpu.VMEM((ROWS, SAMPLES), bf16),
             pltpu.VMEM((N_X * SLOTS, ROWS), bf16),
             pltpu.VMEM(out, bf16),
-            dma((5,)),
-            dma((N_IN,)),
+            dma((7,)),
+            dma((N_IN + 1,)),
         ],
-        [hbm] * 5,
-        hbm,
+        [hbm] * 7,
+        (hbm, hbm),
         60,
-    )(owner_row, cell_row, shift_table, weight_table, traces)
+    )(owner_row, cell_row, gains.reshape(1, count), jnp.asarray(filter_basis()), shift_table, weight_table, traces)
     slots = exchange(slots.reshape(DEVICES, CODES + 8, LANES), ("inline", "xline"))
-    matrix = crossline_filter(gains)
     stacked = call(
         stack_kernel,
         "stack",
@@ -328,17 +342,15 @@
         32,
     )(slots)
     slab = exchange(stacked, "xline")
-    odd = lax.axis_index("inline") % 2
-    order = jnp.stack([odd * HALF, (1 - odd) * LANES])
     return call(
         filter_kernel,
         "crossline",
         jax.ShapeDtypeStruct((SAMPLES // N_IN, 4, N_X * 16), jnp.float32),
         [],
-        [smem, vmem, vmem],
+        [vmem, vmem],
         vmem,
         16,
-    )(order, matrix, slab)
+    )(matrix, slab)
 
 
 def solution(mesh):

time: 81.4 us -> 80.3 us (0.986)
  blocking collectives: 0 us -> 68.2 us
  waiting for transfers between devices: 50.6 us -> 0 us
  starting transfers between devices: 15.9 us -> 0 us
  matrix products: 1.82 us -> 0 us
    all_to_all x0 -> x2, blocking collectives: none -> 68.2 us  [exchange(): return lax.all_to_all(block, axes, split_axis=0, concat_axis=0, tiled=True)]
    all_to_all x2 -> x0, waiting for transfers between devices: 50.6 us -> none  [exchange(): return lax.all_to_all(block, axes, split_axis=0, concat_axis=0, tiled=True)]
    all_to_all x2 -> x0, starting transfers between devices: 15.9 us -> none  [exchange(): return lax.all_to_all(block, axes, split_axis=0, concat_axis=0, tiled=True)]
    dot_general x1 -> x0, matrix products: 1.82 us -> none  [crossline_filter(): lax.dot_general(scaled, jnp.asarray(basis), dims, precision=lax.Precision...]
  transfers between devices with their start and end apart: 2 -> 0, of which waited for: 2 -> 0; matrix products, arithmetic and copies ran while one was open for 2% -> 0% of each run, Pallas kernels for 0% -> 0%
where the time goes in v4:
time: 80.3 us; the launch traced here: 80.1 us
  blocking collectives  68.2 us (85%)
  Pallas kernels  11.9 us (15%)
    all_to_all x2, blocking collectives, exchange(): return lax.all_to_all(block, axes, split_axis=0, concat_axis=0, tiled=True)  68.2 us
    pallas_call x1, Pallas kernels, shards(): call(pack_kernel, 'pack', (jax.ShapeDtypeStruct(out, bf16), jax.ShapeDtyp...  6.93 us
    pallas_call x1, Pallas kernels, shards(): call(stack_kernel, 'stack', jax.ShapeDtypeStruct((N_X, 96, LANES), bf16),...  3.61 us

profile of v4, /device:TPU:0, one launch (start us, length us, event | category | flops | bytes accessed | tf_op | source)
XLA Modules:
  0.0 80.1 jit_solution(7375736611225935586)
XLA Ops:
  0.0 6.9 %pack.1 = (bf16[8,16,104,128]{3,2,1,0:T(8,128)(2,1)}, bf16[256,256]{1,0:T(8,128)(2,1)}) custom-call(s32[1,512]{1,0:T(1,128)} %bitcast.5, s32[1,512]{1,0:T(1,128)} %bitcast.6, f32[1,256]{1,0:T(1,128)} %bitcast.7, f32[256,512]{1,0:T(8,128)} %constant.2.clone.basis_hbm, s32[32,1536]{1,0:T(8,128)} %shift_hbm.1, f32[32,1536]{1,0:T(8,128)} %weight_hbm.1, ...), custom_call_target="tpu_custom_call" | custom-call | tf_op jit(solution)/shard_map/pack/pallas_call | solution.py:310
  6.9 54.3 %all_to_all.10.slots_ref = bf16[128,104,128]{2,1,0:T(8,128)(2,1)S(1)} all-to-all(bf16[128,104,128]{2,1,0:T(8,128)(2,1)} %bitcast.4), channel_id=1, replica_groups=mesh['inline'=8,'xline'=16] {'inline','xline'}, dimensions={0} | all-to-all | bytes 6815744 | tf_op jit(solution)/shard_map/all_to_all | solution.py:300
  61.2 0.0 copy-start
  61.2 3.6 %stack.1 = bf16[16,96,128]{2,1,0:T(8,128)(2,1)S(1)} custom-call(bf16[128,104,128]{2,1,0:T(8,128)(2,1)S(1)} %all_to_all.10.slots_ref), custom_call_target="tpu_custom_call" | custom-call | tf_op jit(solution)/shard_map/stack/pallas_call | solution.py:335
  64.9 13.9 %all_to_all.11.slab_ref = bf16[16,96,128]{2,1,0:T(8,128)(2,1)S(1)} all-to-all(bf16[16,96,128]{2,1,0:T(8,128)(2,1)S(1)} %stack.1), channel_id=1, replica_groups=mesh['inline'=8,'xline'=16] {'xline'}, dimensions={0} | all-to-all | bytes 786432 | tf_op jit(solution)/shard_map/all_to_all | solution.py:300
  78.8 0.0 copy-done
  78.8 1.3 %crossline.1 = f32[192,4,256]{2,1,0:T(4,128)} custom-call(bf16[256,256]{1,0:T(8,128)(2,1)S(1)} %copy-done, bf16[16,96,128]{2,1,0:T(8,128)(2,1)S(1)} %all_to_all.11.slab_ref), custom_call_target="tpu_custom_call" | custom-call | tf_op jit(solution)/shard_map/crossline/pallas_call | solution.py:345
Async XLA Ops:
  61.2 17.5 %copy-start = (bf16[256,256]{1,0:T(8,128)(2,1)S(1)}, bf16[256,256]{1,0:T(8,128)(2,1)}, u32[]{:S(2)}) copy-start(bf16[256,256]{1,0:T(8,128)(2,1)} %get-tuple-element.7.matrix_ref) | copy-start | bytes 393220

commit v5 on v4

--- a/solution.py
+++ b/solution.py
@@ -17,9 +17,9 @@
 N_IN = 8
 N_X = 16
 DEVICES = N_IN * N_X
-SLOTS = 64
-HALF = LANES // 2
-CODES = SLOTS + SLOTS // 2
+SLOTS = 128
+CHUNK = 32
+CODES = 96
 MIB = 1024 * 1024
 
 
@@ -99,11 +99,11 @@
             total = total + jnp.where(same, 1.0, 0.0)
         ranks.append(jnp.sum(total, axis=0, keepdims=True))
     rank = jnp.concatenate(ranks, axis=1).astype(jnp.int32)
-    return (owner_row & (N_X - 1)) * SLOTS + (owner_row >> 4) * 8 + rank
+    return owner_row * 8 + rank
 
 
 def spread(slot, place_ref):
-    for m in range(N_X * SLOTS // LANES):
+    for m in range(N_IN * SLOTS // LANES):
         here = iota((LANES, ROWS), 0) + m * LANES == slot
         place_ref[m * LANES : (m + 1) * LANES, :] = jnp.where(here, 1.0, 0.0).astype(jnp.bfloat16)
 
@@ -143,49 +143,51 @@
     spread(slot, place_ref)
     arrivals[1].wait()
     code = ((slot >> 3) & 1) * LANES + cell_ref[...] + 1
-    line = (slot >> 6) * 8 + ((slot >> 4) & 3)
-    held = jnp.where(iota((LANES, ROWS), 0) == line, code.astype(jnp.float32), 0.0).astype(jnp.bfloat16)
+    lines = N_IN * 8
+    held = jnp.where(iota((lines, ROWS), 0) == slot >> 4, code.astype(jnp.float32), 0.0).astype(jnp.bfloat16)
     lanes = jnp.where((iota((LANES, ROWS), 0) & 15) == (slot & 15), 1.0, 0.0).astype(jnp.bfloat16)
     codes = lax.dot_general(
         held, lanes, (((1,), (1,)), ((), ())), preferred_element_type=jnp.float32
     ).astype(jnp.bfloat16)
     for x in range(N_X):
         for i in range(N_IN):
-            out_ref[i, x, CODES : CODES + 8, :] = codes[x * 8 : (x + 1) * 8]
+            out_ref[i, x, CODES : CODES + 8, :] = codes[x // 2 * 8 : x // 2 * 8 + 8]
     for copy in arrivals[2:]:
         copy.wait()
     matrix_ref[...] = crossline_filter(gains_ref[...], basis_ref[...])
     departures[N_IN].start()
-    low = iota((SLOTS // 2, LANES), 1) < HALF
-
-    def place_pair(n):
+    chunk = iota((CHUNK, LANES), 1) >> 5
+
+    def place(n):
         result = jnp.dot(
-            place_ref[...], moved_ref[:, 2 * n * LANES : 2 * (n + 1) * LANES], preferred_element_type=jnp.float32
+            place_ref[...], moved_ref[:, 3 * n * LANES : 3 * (n + 1) * LANES], preferred_element_type=jnp.float32
         )
-        for k in (2 * n, 2 * n + 1):
-            even = 2 * (k // 3)
-            for x in range(N_X):
-                block = result[x * SLOTS : (x + 1) * SLOTS, (k - 2 * n) * LANES : (k - 2 * n + 1) * LANES]
-                if k % 3 != 1:
-                    out_ref[even + k % 3 // 2, x, 0:SLOTS, :] = block.astype(jnp.bfloat16)
-                    continue
-                first, second = block[: SLOTS // 2], block[SLOTS // 2 :]
-                out_ref[even, x, SLOTS:CODES, :] = jnp.where(
-                    low, first, pltpu.roll(second, HALF, 1)
-                ).astype(jnp.bfloat16)
-                out_ref[even + 1, x, SLOTS:CODES, :] = jnp.where(
-                    low, pltpu.roll(first, HALF, 1), second
-                ).astype(jnp.bfloat16)
-            if k % 3:
-                departures[even + k % 3 - 1].start()
+        for g in range(N_IN):
+            def part(quarter, unit):
+                rows = slice(g * SLOTS + quarter * CHUNK, g * SLOTS + (quarter + 1) * CHUNK)
+                a, b, c = (result[rows, k * LANES : (k + 1) * LANES] for k in range(3))
+                if unit == 1:
+                    return jnp.where(chunk == 3, a, b)
+                if unit == 2:
+                    return jnp.where(chunk == 0, c, b)
+                return c if unit else a
+
+            for unit in range(4):
+                last = part(3, unit)
+                for q in range(3):
+                    out_ref[2 * n + unit // 2, 2 * g + unit % 2, q * CHUNK : (q + 1) * CHUNK, :] = jnp.where(
+                        chunk == 3 - unit, pltpu.roll(last, CHUNK * (3 - q), 1), part(q, unit)
+                    ).astype(jnp.bfloat16)
+        departures[2 * n].start()
+        departures[2 * n + 1].start()
 
     def all_tiles(narrow):
         refs = x_ref, shift_ref, weight_ref, places_ref, moved_ref
 
         if narrow:
-            for n in range(TILES // 2 + 1):
-                if n < TILES // 2:
-                    for k in (2 * n, 2 * n + 1):
+            for n in range(TILES // 3 + 1):
+                if n < TILES // 3:
+                    for k in range(3 * n, 3 * n + 3):
                         for c in range(CLASSES):
                             moveout(
                                 True, k, c,
@@ -193,7 +195,7 @@
                                 slice(c * GROUP, (c + 1) * GROUP), *refs,
                             )
                 if n:
-                    place_pair(n - 1)
+                    place(n - 1)
             return
 
         def step(e, carry):
@@ -209,8 +211,8 @@
             return carry
 
         lax.fori_loop(0, CLASSES // 8, step, 0)
-        for n in range(TILES // 2):
-            place_pair(n)
+        for n in range(TILES // 3):
+            place(n)
 
     narrow = table_places(shift_ref, places_ref)
     pl.when(narrow)(lambda: all_tiles(True))
@@ -219,7 +221,14 @@
         copy.wait()
 
 
-def stack_kernel(slots_ref, out_hbm, select_ref, out_ref, out_sem):
+def units():
+    half = lax.axis_index("xline") & 1
+    first = 2 * (lax.axis_index("inline") & 1)
+    return half, first + half, first + 1 - half
+
+
+def stack_kernel(slots_ref, keep_ref, send_ref, select_ref, stack_ref):
+    half, unit, _ = units()
     bins = (iota((2 * LANES, LANES), 0) + 1).astype(jnp.float32).astype(jnp.bfloat16)
     depth = DEVICES * 16
     ones = jnp.ones((depth, LANES), jnp.bfloat16)
@@ -231,12 +240,12 @@
             codes = slots_ref[8 * j + g, CODES : CODES + 8, :].astype(jnp.float32)
             line = jnp.where(mine, codes, line)
         lines.append(line)
-    low = iota((32, LANES), 1) < HALF
-
-    def departure(p):
-        return pltpu.make_async_copy(out_ref.at[4 * p : 4 * p + 4], out_hbm.at[4 * p : 4 * p + 4], out_sem.at[p])
-
-    for p in range(4):
+    time = ((iota((2 * LANES, LANES), 1) >> 5) + unit) & 3
+
+    def rows_of(first):
+        return slots_ref[:, first : first + 16, :].reshape(depth, LANES)
+
+    for p in range(8):
         for j in range(DEVICES // 8):
             row = jnp.broadcast_to(lines[j][p : p + 1], (16, LANES)).astype(jnp.bfloat16)
             row = jnp.concatenate([row] * 16, axis=0)
@@ -244,44 +253,48 @@
                 bins == row, jnp.bfloat16(1), jnp.bfloat16(0)
             )
         select = select_ref[...]
-        full = slots_ref[:, 16 * p : 16 * p + 16, :].reshape(depth, LANES)
-        q = p % 2
-        half = slots_ref[:, SLOTS + 16 * q : SLOTS + 16 * q + 16, :].reshape(depth, LANES)
-        sums = jnp.dot(select, jnp.concatenate([full, ones], axis=1), preferred_element_type=jnp.float32)
-        fold = jnp.maximum(sums[:, LANES:], 1.0)
-        mean = sums[:, :LANES] / fold
-        part = jnp.dot(select, half, preferred_element_type=jnp.float32) / fold
-        for x in range(4):
-            rows = slice(64 * x, 64 * x + 64)
-            out_ref[4 * p + x, 0:64, :] = mean[rows].astype(jnp.bfloat16)
-            first, second = part[64 * x : 64 * x + 32], part[64 * x + 32 : 64 * x + 64]
-            if p < 2:
-                packed = jnp.where(low, first, pltpu.roll(second, HALF, 1))
-            else:
-                packed = jnp.where(low, pltpu.roll(first, HALF, 1), second)
-            out_ref[4 * p + x, 64:96, :] = packed.astype(jnp.bfloat16)
-        departure(p).start()
-    for p in range(4):
-        departure(p).wait()
-
-
-def filter_kernel(matrix_ref, slab_ref, out_ref):
-    odd = lax.axis_index("inline") & 1
-    whole_at, shared_at = odd * HALF, (1 - odd) * LANES
+
+        def sums_of(a, b):
+            both = jnp.dot(select, jnp.concatenate([a, b], axis=1), preferred_element_type=jnp.float32)
+            return both[:, :LANES], both[:, LANES:]
+
+        if p < 6:
+            sums, fold = sums_of(rows_of(16 * p), ones)
+        else:
+            first, second = sums_of(rows_of(16 * (p - 6)), rows_of(CHUNK + 16 * (p - 6)))
+            third, fold = sums_of(rows_of(2 * CHUNK + 16 * (p - 6)), ones)
+            first, second, third = (
+                pltpu.roll(part, CHUNK * (q + 1), 1) for q, part in enumerate((first, second, third))
+            )
+            sums = jnp.where(time == 0, first, jnp.where(time == 1, second, third))
+        mean = (sums / jnp.maximum(fold, 1.0)).astype(jnp.bfloat16)
+        stack_ref[2 * p] = mean[:LANES]
+        stack_ref[2 * p + 1] = mean[LANES:]
+    mine, other = pl.multiple_of(half * 64, 64), pl.multiple_of((1 - half) * 64, 64)
+    send_ref[...] = stack_ref[:, pl.ds(other, 64), :]
+    keep_ref[...] = stack_ref[:, pl.ds(mine, 64), :]
+
+
+def filter_kernel(matrix_ref, keep_ref, received_ref, out_ref):
+    half, own, neighbour = units()
     matrix = matrix_ref[...]
-    count = N_X * 16
-
-    def apply(block):
-        return lax.dot_general(block, matrix, (((0,), (0,)), ((), ())), preferred_element_type=jnp.float32)
-
-    for i in range(4):
-        full = slab_ref[:, 16 * i : 16 * i + 16, :].reshape(count, LANES)
-        out_ref[pl.ds(whole_at, LANES), i, :] = apply(full)
-    for i in range(2):
-        pair = slab_ref[:, 64 + 16 * i : 80 + 16 * i, :].reshape(count, LANES)
-        both = apply(pair)
-        out_ref[pl.ds(shared_at, HALF), i, :] = both[:HALF]
-        out_ref[pl.ds(shared_at, HALF), i + 2, :] = both[HALF:]
+    for ref, start, unit in ((keep_ref, 96 * half, own), (received_ref, 96 * (1 - half), neighbour)):
+        results = [
+            lax.dot_general(
+                ref[:, 16 * i : 16 * i + 16, :].reshape(N_X * 16, LANES),
+                matrix,
+                (((0,), (0,)), ((), ())),
+                preferred_element_type=jnp.float32,
+            )
+            for i in range(4)
+        ]
+        for m in range(4):
+            time = (m + unit) & 3
+
+            @pl.when(time < 3)
+            def _():
+                for i in range(4):
+                    out_ref[pl.ds(start + CHUNK * time, CHUNK), i, :] = results[i][m * CHUNK : (m + 1) * CHUNK]
 
 
 def call(kernel, name, out_shape, scratch, in_specs, out_specs, mib):
@@ -322,7 +335,7 @@
             pltpu.VMEM((count, count), bf16),
             pltpu.VMEM((4, CLASSES, SAMPLES), jnp.int32),
             pltpu.VMEM((ROWS, SAMPLES), bf16),
-            pltpu.VMEM((N_X * SLOTS, ROWS), bf16),
+            pltpu.VMEM((N_IN * SLOTS, ROWS), bf16),
             pltpu.VMEM(out, bf16),
             dma((7,)),
             dma((N_IN + 1,)),
@@ -332,25 +345,26 @@
         60,
     )(owner_row, cell_row, gains.reshape(1, count), jnp.asarray(filter_basis()), shift_table, weight_table, traces)
     slots = exchange(slots.reshape(DEVICES, CODES + 8, LANES), ("inline", "xline"))
-    stacked = call(
+    part = jax.ShapeDtypeStruct((N_X, 64, LANES), bf16)
+    keep, send = call(
         stack_kernel,
         "stack",
-        jax.ShapeDtypeStruct((N_X, 96, LANES), bf16),
-        [pltpu.VMEM((2 * LANES, DEVICES * 16), bf16), pltpu.VMEM((N_X, 96, LANES), bf16), dma((4,))],
+        (part, part),
+        [pltpu.VMEM((2 * LANES, DEVICES * 16), bf16), pltpu.VMEM((N_X, LANES, LANES), bf16)],
         [vmem],
-        hbm,
+        (vmem, vmem),
         32,
     )(slots)
-    slab = exchange(stacked, "xline")
+    received = lax.ppermute(send, "xline", [(x, x ^ 1) for x in range(N_X)])
     return call(
         filter_kernel,
         "crossline",
         jax.ShapeDtypeStruct((SAMPLES // N_IN, 4, N_X * 16), jnp.float32),
         [],
-        [vmem, vmem],
+        [vmem] * 3,
         vmem,
         16,
-    )(matrix, slab)
+    )(matrix, keep, received)
 
 
 def solution(mesh):

time: 80.3 us -> 76.6 us (0.954)
  blocking collectives: 68.2 us -> 54.3 us
  waiting for transfers between devices: 0 us -> 7.33 us
  starting transfers between devices: 0 us -> 1.41 us
  Pallas kernels: 11.9 us -> 12.8 us
    all_to_all x2 -> x1, blocking collectives: 68.2 us -> 54.3 us  [exchange(): return lax.all_to_all(block, axes, split_axis=0, concat_axis=0, tiled=True)]
    ppermute x0 -> x1, waiting for transfers between devices: none -> 7.33 us  [shards(): received = lax.ppermute(send, 'xline', [(x, x ^ 1) for x in range(N_X)])]
    ppermute x0 -> x1, starting transfers between devices: none -> 1.41 us  [shards(): received = lax.ppermute(send, 'xline', [(x, x ^ 1) for x in range(N_X)])]
  transfers between devices with their start and end apart: 0 -> 1, of which waited for: 0 -> 1; matrix products, arithmetic and copies ran while one was open for 0% -> 0% of each run, Pallas kernels for 0% -> 0%
where the time goes in v5:
time: 76.6 us; the launch traced here: 75.8 us
  blocking collectives  54.3 us (71%)
  Pallas kernels  12.8 us (17%)
  waiting for transfers between devices  7.33 us (10%)
  starting transfers between devices  1.41 us (2%)
    all_to_all x1, blocking collectives, exchange(): return lax.all_to_all(block, axes, split_axis=0, concat_axis=0, tiled=True)  54.3 us
    ppermute x1, waiting for transfers between devices, shards(): received = lax.ppermute(send, 'xline', [(x, x ^ 1) for x in range(N_X)])  7.33 us
    pallas_call x1, Pallas kernels, shards(): call(pack_kernel, 'pack', (jax.ShapeDtypeStruct(out, bf16), jax.ShapeDtyp...  7.3 us
    pallas_call x1, Pallas kernels, shards(): call(stack_kernel, 'stack', (part, part), [pltpu.VMEM((2 * LANES, DEVICES...  3.79 us
    pallas_call x1, Pallas kernels, shards(): call(filter_kernel, 'crossline', jax.ShapeDtypeStruct((SAMPLES // N_IN, 4...  1.68 us
  transfers between devices with their start and end apart: 1, of which 1 were waited for; matrix products, arithmetic and copies ran while one was open for 0% of the time, Pallas kernels for 0%

profile of v5, /device:TPU:0, one launch (start us, length us, event | category | flops | bytes accessed | tf_op | source)
XLA Modules:
  0.0 75.8 jit_solution(16507707397868722134)
XLA Ops:
  0.0 7.3 %pack.1 = (bf16[8,16,104,128]{3,2,1,0:T(8,128)(2,1)}, bf16[256,256]{1,0:T(8,128)(2,1)}) custom-call(s32[1,512]{1,0:T(1,128)} %bitcast.5, s32[1,512]{1,0:T(1,128)} %bitcast.6, f32[1,256]{1,0:T(1,128)} %bitcast.7, f32[256,512]{1,0:T(8,128)} %constant.2.clone.basis_hbm, s32[32,1536]{1,0:T(8,128)} %shift_hbm.1, f32[32,1536]{1,0:T(8,128)} %weight_hbm.1, ...), custom_call_target="tpu_custom_call" | custom-call | tf_op jit(solution)/shard_map/pack/pallas_call | solution.py:323
  7.3 54.3 %all_to_all.5.slots_ref = bf16[128,104,128]{2,1,0:T(8,128)(2,1)S(1)} all-to-all(bf16[128,104,128]{2,1,0:T(8,128)(2,1)} %bitcast.4), channel_id=1, replica_groups=mesh['inline'=8,'xline'=16] {'inline','xline'}, dimensions={0} | all-to-all | bytes 6815744 | tf_op jit(solution)/shard_map/all_to_all | solution.py:313
  61.6 0.0 copy-start
  61.6 3.8 %stack.1 = (bf16[16,64,128]{2,1,0:T(8,128)(2,1)S(1)}, bf16[16,64,128]{2,1,0:T(8,128)(2,1)S(1)}) custom-call(bf16[128,104,128]{2,1,0:T(8,128)(2,1)S(1)} %all_to_all.5.slots_ref), custom_call_target="tpu_custom_call" | custom-call | tf_op jit(solution)/shard_map/stack/pallas_call | solution.py:349
  65.4 1.4 %collective-permute-start = (bf16[16,64,128]{2,1,0:T(8,128)(2,1)S(1)}, bf16[16,64,128]{2,1,0:T(8,128)(2,1)S(1)}, u32[]{:S(2)}, u32[]{:S(2)}) collective-permute-start(bf16[16,64,128]{2,1,0:T(8,128)(2,1)S(1)} %get-tuple-element.12), channel_id=1, source_target_pairs={{0,1},{1,0},{2,3},{3,2},{4,5},{5,4},{6,7},{7,6},{8,9},{9,8},{10,11... | collective-permute-start | bytes 786440 | tf_op jit(solution)/shard_map/ppermute | solution.py:358
  66.8 7.3 %collective-permute-done.received_ref = bf16[16,64,128]{2,1,0:T(8,128)(2,1)S(1)} collective-permute-done((bf16[16,64,128]{2,1,0:T(8,128)(2,1)S(1)}, bf16[16,64,128]{2,1,0:T(8,128)(2,1)S(1)}, u32[]{:S(2)}, u32[]{:S(2)}) %collective-permute-start) | collective-permute-done | bytes 262176 | tf_op jit(solution)/shard_map/ppermute | solution.py:358
  74.1 0.0 copy-done
  74.2 1.7 %crossline.1 = f32[192,4,256]{2,1,0:T(4,128)} custom-call(bf16[256,256]{1,0:T(8,128)(2,1)S(1)} %copy-done, bf16[16,64,128]{2,1,0:T(8,128)(2,1)S(1)} %get-tuple-element.11.keep_ref, bf16[16,64,128]{2,1,0:T(8,128)(2,1)S(1)} %collective-permute-done.received_ref), custom_call_target="tpu_custom_call" | custom-call | tf_op jit(solution)/shard_map/crossline/pallas_call | solution.py:359
Async XLA Ops:
  61.6 12.5 %copy-start = (bf16[256,256]{1,0:T(8,128)(2,1)S(1)}, bf16[256,256]{1,0:T(8,128)(2,1)}, u32[]{:S(2)}) copy-start(bf16[256,256]{1,0:T(8,128)(2,1)} %get-tuple-element.9.matrix_ref) | copy-start | bytes 393220
  65.4 8.7 %collective-permute-start = (bf16[16,64,128]{2,1,0:T(8,128)(2,1)S(1)}, bf16[16,64,128]{2,1,0:T(8,128)(2,1)S(1)}, u32[]{:S(2)}, u32[]{:S(2)}) collective-permute-start(bf16[16,64,128]{2,1,0:T(8,128)(2,1)S(1)} %get-tuple-element.12), channel_id=1, source_target_pairs={{0,1},{1,0},{2,3},{3,2},{4,5},{5,4},{6,7},{7,6},{8,9},{9,8},{10,11... | collective-permute-start | bytes 786440 | tf_op jit(solution)/shard_map/ppermute | solution.py:358

commit v6 on v5

--- a/solution.py
+++ b/solution.py
@@ -227,7 +227,7 @@
     return half, first + half, first + 1 - half
 
 
-def stack_kernel(slots_ref, keep_ref, send_ref, select_ref, stack_ref):
+def stack_kernel(pairs, slots_ref, keep_ref, send_ref, select_ref, halves_ref):
     half, unit, _ = units()
     bins = (iota((2 * LANES, LANES), 0) + 1).astype(jnp.float32).astype(jnp.bfloat16)
     depth = DEVICES * 16
@@ -241,11 +241,12 @@
             line = jnp.where(mine, codes, line)
         lines.append(line)
     time = ((iota((2 * LANES, LANES), 1) >> 5) + unit) & 3
+    free = ((iota((16, LANES), 1) >> 5) + unit) & 3 == 3
 
     def rows_of(first):
         return slots_ref[:, first : first + 16, :].reshape(depth, LANES)
 
-    for p in range(8):
+    for p in pairs:
         for j in range(DEVICES // 8):
             row = jnp.broadcast_to(lines[j][p : p + 1], (16, LANES)).astype(jnp.bfloat16)
             row = jnp.concatenate([row] * 16, axis=0)
@@ -267,37 +268,54 @@
                 pltpu.roll(part, CHUNK * (q + 1), 1) for q, part in enumerate((first, second, third))
             )
             sums = jnp.where(time == 0, first, jnp.where(time == 1, second, third))
-        mean = (sums / jnp.maximum(fold, 1.0)).astype(jnp.bfloat16)
-        stack_ref[2 * p] = mean[:LANES]
-        stack_ref[2 * p + 1] = mean[LANES:]
-    mine, other = pl.multiple_of(half * 64, 64), pl.multiple_of((1 - half) * 64, 64)
-    send_ref[...] = stack_ref[:, pl.ds(other, 64), :]
-    keep_ref[...] = stack_ref[:, pl.ds(mine, 64), :]
-
-
-def filter_kernel(matrix_ref, keep_ref, received_ref, out_ref):
-    half, own, neighbour = units()
+        mean = sums / jnp.maximum(fold, 1.0)
+        for o in range(2):
+            for h in range(2):
+                four = [mean[o * LANES + h * 64 + 16 * i : o * LANES + h * 64 + 16 * i + 16] for i in range(4)]
+                for i in range(3):
+                    halves_ref[h, 2 * (p - pairs[0]) + o, 16 * i : 16 * i + 16, :] = jnp.where(
+                        free, pltpu.roll(four[3], CHUNK * (3 - i), 1), four[i]
+                    ).astype(jnp.bfloat16)
+    send_ref[...] = halves_ref[1 - half]
+    keep_ref[...] = halves_ref[half]
+
+
+def filter_kernel(own, matrix_ref, first_ref, second_ref, *rest):
+    out_hbm, slab_ref, sem = rest[-3:]
+    half, own_unit, neighbour_unit = units()
+    start, unit = (96 * half, own_unit) if own else (96 * (1 - half), neighbour_unit)
     matrix = matrix_ref[...]
-    for ref, start, unit in ((keep_ref, 96 * half, own), (received_ref, 96 * (1 - half), neighbour)):
-        results = [
+    results = []
+    for i in range(3):
+        rows = [ref[:, 16 * i : 16 * i + 16, :].reshape(-1, LANES) for ref in (first_ref, second_ref)]
+        results.append(
             lax.dot_general(
-                ref[:, 16 * i : 16 * i + 16, :].reshape(N_X * 16, LANES),
+                jnp.concatenate(rows, axis=0),
                 matrix,
                 (((0,), (0,)), ((), ())),
                 preferred_element_type=jnp.float32,
             )
-            for i in range(4)
-        ]
-        for m in range(4):
-            time = (m + unit) & 3
-
-            @pl.when(time < 3)
-            def _():
-                for i in range(4):
-                    out_ref[pl.ds(start + CHUNK * time, CHUNK), i, :] = results[i][m * CHUNK : (m + 1) * CHUNK]
-
-
-def call(kernel, name, out_shape, scratch, in_specs, out_specs, mib):
+        )
+    for m in range(4):
+        time = (m + unit) & 3
+        parts = [result[m * CHUNK : (m + 1) * CHUNK] for result in results]
+
+        @pl.when(time < 3)
+        def _():
+            for i in range(3):
+                slab_ref[pl.ds(CHUNK * time, CHUNK), i, :] = parts[i]
+
+        @pl.when(time == 3)
+        def _():
+            for i in range(3):
+                slab_ref[CHUNK * i : CHUNK * (i + 1), 3, :] = parts[i]
+
+    copy = pltpu.make_async_copy(slab_ref, out_hbm.at[pl.ds(start, 96)], sem)
+    copy.start()
+    copy.wait()
+
+
+def call(kernel, name, out_shape, scratch, in_specs, out_specs, mib, aliases=None):
     return pl.pallas_call(
         kernel,
         out_shape=out_shape,
@@ -305,6 +323,7 @@
         name=name,
         in_specs=in_specs,
         out_specs=out_specs,
+        input_output_aliases=aliases or {},
         compiler_params=pltpu.CompilerParams(vmem_limit_bytes=mib * MIB),
     )
 
@@ -345,26 +364,35 @@
         60,
     )(owner_row, cell_row, gains.reshape(1, count), jnp.asarray(filter_basis()), shift_table, weight_table, traces)
     slots = exchange(slots.reshape(DEVICES, CODES + 8, LANES), ("inline", "xline"))
-    part = jax.ShapeDtypeStruct((N_X, 64, LANES), bf16)
-    keep, send = call(
-        stack_kernel,
-        "stack",
-        (part, part),
-        [pltpu.VMEM((2 * LANES, DEVICES * 16), bf16), pltpu.VMEM((N_X, LANES, LANES), bf16)],
-        [vmem],
-        (vmem, vmem),
-        32,
-    )(slots)
-    received = lax.ppermute(send, "xline", [(x, x ^ 1) for x in range(N_X)])
+    keep, received = [], []
+    for pairs in (range(6), range(6, 8)):
+        part = jax.ShapeDtypeStruct((2 * len(pairs), 48, LANES), bf16)
+        kept, send = call(
+            functools.partial(stack_kernel, pairs),
+            f"stack_{pairs[0]}",
+            (part, part),
+            [pltpu.VMEM((2 * LANES, DEVICES * 16), bf16), pltpu.VMEM((2, *part.shape), bf16)],
+            [vmem],
+            (vmem, vmem),
+            32,
+        )(slots)
+        keep.append(kept)
+        received.append(lax.ppermute(send, "xline", [(x, x ^ 1) for x in range(N_X)]))
+    result = jax.ShapeDtypeStruct((SAMPLES // N_IN, 4, count), jnp.float32)
+    scratch = [pltpu.VMEM((96, 4, count), jnp.float32), dma]
+    own = call(
+        functools.partial(filter_kernel, True), "crossline_own", result, scratch, [vmem] * 3, hbm, 16
+    )(matrix, *keep)
     return call(
-        filter_kernel,
-        "crossline",
-        jax.ShapeDtypeStruct((SAMPLES // N_IN, 4, N_X * 16), jnp.float32),
-        [],
-        [vmem] * 3,
-        vmem,
+        functools.partial(filter_kernel, False),
+        "crossline_received",
+        result,
+        scratch,
+        [vmem] * 3 + [hbm],
+        hbm,
         16,
-    )(matrix, keep, received)
+        {3: 0},
+    )(matrix, *received, own)
 
 
 def solution(mesh):

time: 76.6 us -> 73.4 us (0.958)
  waiting for transfers between devices: 7.33 us -> 2.39 us
  Pallas kernels: 12.8 us -> 13.7 us
    ppermute x1 -> x2, waiting for transfers between devices: 7.33 us -> 2.39 us  [shards(): lax.ppermute(send, 'xline', [(x, x ^ 1) for x in range(N_X)])]
    pallas_call x2 -> x4, Pallas kernels: 5.48 us -> 6.41 us  [the longest x2 4.1 us: shards(): call(functools.partial(stack_kernel, pairs), f'stack_{pairs[0]}', (part,...]
    ppermute x1 -> x2, starting transfers between devices: 1.41 us -> 2.17 us  [shards(): lax.ppermute(send, 'xline', [(x, x ^ 1) for x in range(N_X)])]
  transfers between devices with their start and end apart: 1 -> 2, of which waited for: 1 -> 1; matrix products, arithmetic and copies ran while one was open for 0% -> 0% of each run, Pallas kernels for 0% -> 4%
where the time goes in v6:
time: 73.4 us; the launch traced here: 72.6 us
  blocking collectives  54.3 us (74%)
  Pallas kernels  13.7 us (19%)
  waiting for transfers between devices  2.39 us (3%)
  starting transfers between devices  2.17 us (3%)
    all_to_all x1, blocking collectives, exchange(): return lax.all_to_all(block, axes, split_axis=0, concat_axis=0, tiled=True)  54.3 us
    pallas_call x1, Pallas kernels, shards(): call(pack_kernel, 'pack', (jax.ShapeDtypeStruct(out, bf16), jax.ShapeDtyp...  7.31 us
    pallas_call x2, Pallas kernels, shards(): call(functools.partial(stack_kernel, pairs), f'stack_{pairs[0]}', (part,...  4.1 us
    ppermute x2, waiting for transfers between devices, shards(): lax.ppermute(send, 'xline', [(x, x ^ 1) for x in range(N_X)])  2.39 us
    ppermute x2, starting transfers between devices, shards(): lax.ppermute(send, 'xline', [(x, x ^ 1) for x in range(N_X)])  2.17 us
  transfers between devices with their start and end apart: 2, of which 1 were waited for; matrix products, arithmetic and copies ran while one was open for 0% of the time, Pallas kernels for 4%

profile of v6, /device:TPU:0, one launch (start us, length us, event | category | flops | bytes accessed | tf_op | source)
XLA Modules:
  0.0 72.6 jit_solution(14376612391948608291)
XLA Ops:
  0.0 7.3 %pack.1 = (bf16[8,16,104,128]{3,2,1,0:T(8,128)(2,1)}, bf16[256,256]{1,0:T(8,128)(2,1)}) custom-call(s32[1,512]{1,0:T(1,128)} %bitcast.5, s32[1,512]{1,0:T(1,128)} %bitcast.6, f32[1,256]{1,0:T(1,128)} %bitcast.7, f32[256,512]{1,0:T(8,128)} %constant.2.clone.basis_hbm, s32[32,1536]{1,0:T(8,128)} %shift_hbm.1, f32[32,1536]{1,0:T(8,128)} %weight_hbm.1, ...), custom_call_target="tpu_custom_call" | custom-call | tf_op jit(solution)/shard_map/pack/pallas_call | solution.py:342
  7.3 54.3 %all_to_all.5.slots_ref = bf16[128,104,128]{2,1,0:T(8,128)(2,1)S(1)} all-to-all(bf16[128,104,128]{2,1,0:T(8,128)(2,1)} %bitcast.4), channel_id=1, replica_groups=mesh['inline'=8,'xline'=16] {'inline','xline'}, dimensions={0} | all-to-all | bytes 6815744 | tf_op jit(solution)/shard_map/all_to_all | solution.py:332
  61.6 0.0 copy-start
  61.6 2.5 %stack_0.1 = (bf16[12,48,128]{2,1,0:T(8,128)(2,1)S(1)}, bf16[12,48,128]{2,1,0:T(8,128)(2,1)S(1)}) custom-call(bf16[128,104,128]{2,1,0:T(8,128)(2,1)S(1)} %all_to_all.5.slots_ref), custom_call_target="tpu_custom_call" | custom-call | tf_op jit(solution)/shard_map/stack_0/pallas_call | solution.py:370
  64.1 1.4 %collective-permute-start = (bf16[12,48,128]{2,1,0:T(8,128)(2,1)S(1)}, bf16[12,48,128]{2,1,0:T(8,128)(2,1)S(1)}, u32[]{:S(2)}, u32[]{:S(2)}) collective-permute-start(bf16[12,48,128]{2,1,0:T(8,128)(2,1)S(1)} %get-tuple-element.13), channel_id=1, source_target_pairs={{0,1},{1,0},{2,3},{3,2},{4,5},{5,4},{6,7},{7,6},{8,9},{9,8},{10,11... | collective-permute-start | bytes 442376 | tf_op jit(solution)/shard_map/ppermute | solution.py:380
  65.5 1.6 %stack_6.1 = (bf16[4,48,128]{2,1,0:T(8,128)(2,1)S(1)}, bf16[4,48,128]{2,1,0:T(8,128)(2,1)S(1)}) custom-call(bf16[128,104,128]{2,1,0:T(8,128)(2,1)S(1)} %all_to_all.5.slots_ref), custom_call_target="tpu_custom_call" | custom-call | tf_op jit(solution)/shard_map/stack_6/pallas_call | solution.py:370
  67.1 0.8 %collective-permute-start.1 = (bf16[4,48,128]{2,1,0:T(8,128)(2,1)S(1)}, bf16[4,48,128]{2,1,0:T(8,128)(2,1)S(1)}, u32[]{:S(2)}, u32[]{:S(2)}) collective-permute-start(bf16[4,48,128]{2,1,0:T(8,128)(2,1)S(1)} %get-tuple-element.14), channel_id=1, source_target_pairs={{0,1},{1,0},{2,3},{3,2},{4,5},{5,4},{6,7},{7,6},{8,9},{9,8},{10,11... | collective-permute-start | bytes 147464 | tf_op jit(solution)/shard_map/ppermute | solution.py:380
  67.9 0.0 copy-done
  67.9 1.2 %crossline_own.1.rest_0_ = f32[192,4,256]{2,1,0:T(4,128)} custom-call(bf16[256,256]{1,0:T(8,128)(2,1)S(1)} %copy-done, bf16[12,48,128]{2,1,0:T(8,128)(2,1)S(1)} %get-tuple-element.15.first_ref, bf16[4,48,128]{2,1,0:T(8,128)(2,1)S(1)} %get-tuple-element.16.second_ref), custom_call_target="tpu_custom_call" | custom-call | tf_op jit(solution)/shard_map/crossline_own/pallas_call | solution.py:383
  69.1 2.4 %collective-permute-done.1.second_ref = bf16[4,48,128]{2,1,0:T(8,128)(2,1)S(1)} collective-permute-done((bf16[4,48,128]{2,1,0:T(8,128)(2,1)S(1)}, bf16[4,48,128]{2,1,0:T(8,128)(2,1)S(1)}, u32[]{:S(2)}, u32[]{:S(2)}) %collective-permute-start.1) | collective-permute-done | bytes 49184 | tf_op jit(solution)/shard_map/ppermute | solution.py:380
  71.5 0.0 collective-permute-done.first_ref
  71.5 1.2 %crossline_received.1 = f32[192,4,256]{2,1,0:T(4,128)} custom-call(bf16[256,256]{1,0:T(8,128)(2,1)S(1)} %copy-done, bf16[12,48,128]{2,1,0:T(8,128)(2,1)S(1)} %collective-permute-done.first_ref, bf16[4,48,128]{2,1,0:T(8,128)(2,1)S(1)} %collective-permute-done.1.second_ref, f32[192,4,256]{2,1,0:T(4,128)} %crossline_own.1.rest_0_), custom_call_target="tpu_custom_call", output_to_operand_aliasing={{}: (3, {})} | custom-call | tf_op jit(solution)/shard_map/crossline_received/pallas_call | solution.py:386
Async XLA Ops:
  61.6 6.3 %copy-start = (bf16[256,256]{1,0:T(8,128)(2,1)S(1)}, bf16[256,256]{1,0:T(8,128)(2,1)}, u32[]{:S(2)}) copy-start(bf16[256,256]{1,0:T(8,128)(2,1)} %get-tuple-element.11.matrix_ref) | copy-start | bytes 393220
  64.1 7.3 %collective-permute-start = (bf16[12,48,128]{2,1,0:T(8,128)(2,1)S(1)}, bf16[12,48,128]{2,1,0:T(8,128)(2,1)S(1)}, u32[]{:S(2)}, u32[]{:S(2)}) collective-permute-start(bf16[12,48,128]{2,1,0:T(8,128)(2,1)S(1)} %get-tuple-element.13), channel_id=1, source_target_pairs={{0,1},{1,0},{2,3},{3,2},{4,5},{5,4},{6,7},{7,6},{8,9},{9,8},{10,11... | collective-permute-start | bytes 442376 | tf_op jit(solution)/shard_map/ppermute | solution.py:380
  67.1 4.3 %collective-permute-start.1 = (bf16[4,48,128]{2,1,0:T(8,128)(2,1)S(1)}, bf16[4,48,128]{2,1,0:T(8,128)(2,1)S(1)}, u32[]{:S(2)}, u32[]{:S(2)}) collective-permute-start(bf16[4,48,128]{2,1,0:T(8,128)(2,1)S(1)} %get-tuple-element.14), channel_id=1, source_target_pairs={{0,1},{1,0},{2,3},{3,2},{4,5},{5,4},{6,7},{7,6},{8,9},{9,8},{10,11... | collective-permute-start | bytes 147464 | tf_op jit(solution)/shard_map/ppermute | solution.py:380

commit v7 on v6

--- a/solution.py
+++ b/solution.py
@@ -19,7 +19,8 @@
 DEVICES = N_IN * N_X
 SLOTS = 128
 CHUNK = 32
-CODES = 96
+BLOCK = (25, 4, LANES)
+CODES = 24
 MIB = 1024 * 1024
 
 
@@ -115,27 +116,25 @@
     return np.concatenate([np.cos(phase), np.sin(phase)], axis=1).astype(np.float32)
 
 
-def crossline_filter(gains, basis):
-    count = basis.shape[0]
+def matrix_kernel(gains_ref, basis_ref, matrix_ref):
+    gains, basis = gains_ref[...], basis_ref[...]
     scaled = basis * jnp.concatenate([gains, gains], axis=1)
     dims = (((1,), (1,)), ((), ()))
     product = lax.dot_general(
         scaled, basis, dims, precision=lax.Precision.HIGHEST, preferred_element_type=jnp.float32
     )
-    return (product / count).astype(jnp.bfloat16)
+    matrix_ref[...] = (product / basis.shape[0]).astype(jnp.bfloat16)
 
 
 def pack_kernel(
-    owner_hbm, cell_hbm, gains_hbm, basis_hbm, shift_hbm, weight_hbm, x_hbm, out_hbm, matrix_hbm,
-    owner_ref, cell_ref, gains_ref, basis_ref, shift_ref, weight_ref, x_ref, matrix_ref, places_ref, moved_ref, place_ref, out_ref, in_sem, out_sem,
+    owner_hbm, cell_hbm, shift_hbm, weight_hbm, x_hbm, out_hbm,
+    owner_ref, cell_ref, shift_ref, weight_ref, x_ref, places_ref, moved_ref, place_ref, out_ref, in_sem, out_sem,
 ):
     arrays = [
         (owner_hbm, owner_ref), (cell_hbm, cell_ref), (shift_hbm, shift_ref), (weight_hbm, weight_ref), (x_hbm, x_ref),
-        (gains_hbm, gains_ref), (basis_hbm, basis_ref),
     ]
     arrivals = [pltpu.make_async_copy(a, b, in_sem.at[n]) for n, (a, b) in enumerate(arrays)]
     departures = [pltpu.make_async_copy(out_ref.at[i], out_hbm.at[i], out_sem.at[i]) for i in range(N_IN)]
-    departures.append(pltpu.make_async_copy(matrix_ref, matrix_hbm, out_sem.at[N_IN]))
     for copy in arrivals:
         copy.start()
     arrivals[0].wait()
@@ -143,19 +142,17 @@
     spread(slot, place_ref)
     arrivals[1].wait()
     code = ((slot >> 3) & 1) * LANES + cell_ref[...] + 1
-    lines = N_IN * 8
-    held = jnp.where(iota((lines, ROWS), 0) == slot >> 4, code.astype(jnp.float32), 0.0).astype(jnp.bfloat16)
-    lanes = jnp.where((iota((LANES, ROWS), 0) & 15) == (slot & 15), 1.0, 0.0).astype(jnp.bfloat16)
+    lines = N_IN * 4
+    held = jnp.where(iota((lines, ROWS), 0) == slot >> 5, code.astype(jnp.float32), 0.0).astype(jnp.bfloat16)
+    lanes = jnp.where((iota((LANES, ROWS), 0) & 31) == (slot & 31), 1.0, 0.0).astype(jnp.bfloat16)
     codes = lax.dot_general(
         held, lanes, (((1,), (1,)), ((), ())), preferred_element_type=jnp.float32
-    ).astype(jnp.bfloat16)
+    ).astype(jnp.bfloat16).reshape(N_IN, 4, LANES)
     for x in range(N_X):
         for i in range(N_IN):
-            out_ref[i, x, CODES : CODES + 8, :] = codes[x // 2 * 8 : x // 2 * 8 + 8]
+            out_ref[i, x, CODES] = codes[x // 2]
     for copy in arrivals[2:]:
         copy.wait()
-    matrix_ref[...] = crossline_filter(gains_ref[...], basis_ref[...])
-    departures[N_IN].start()
     chunk = iota((CHUNK, LANES), 1) >> 5
 
     def place(n):
@@ -175,9 +172,10 @@
             for unit in range(4):
                 last = part(3, unit)
                 for q in range(3):
-                    out_ref[2 * n + unit // 2, 2 * g + unit % 2, q * CHUNK : (q + 1) * CHUNK, :] = jnp.where(
-                        chunk == 3 - unit, pltpu.roll(last, CHUNK * (3 - q), 1), part(q, unit)
-                    ).astype(jnp.bfloat16)
+                    block = jnp.where(chunk == 3 - unit, pltpu.roll(last, CHUNK * (3 - q), 1), part(q, unit))
+                    out_ref[2 * n + unit // 2, 2 * g + unit % 2, 8 * q : 8 * q + 8] = block.astype(
+                        jnp.bfloat16
+                    ).reshape(8, 4, LANES)
         departures[2 * n].start()
         departures[2 * n + 1].start()
 
@@ -232,23 +230,25 @@
     bins = (iota((2 * LANES, LANES), 0) + 1).astype(jnp.float32).astype(jnp.bfloat16)
     depth = DEVICES * 16
     ones = jnp.ones((depth, LANES), jnp.bfloat16)
+    group = iota((4, LANES), 1) >> 4
     lines = []
     for j in range(DEVICES // 8):
-        line = jnp.zeros((8, LANES), jnp.float32)
+        here = there = jnp.zeros((4, LANES), jnp.float32)
         for g in range(8):
-            mine = (iota((8, LANES), 1) >> 4) == g
-            codes = slots_ref[8 * j + g, CODES : CODES + 8, :].astype(jnp.float32)
-            line = jnp.where(mine, codes, line)
-        lines.append(line)
+            codes = slots_ref[8 * j + g, CODES].astype(jnp.float32)
+            here = jnp.where(group == g, codes, here)
+            there = jnp.where(group == (g - 1) % 8, codes, there)
+        there = pltpu.roll(there, 16, 1)
+        lines.append([jnp.where(group & 1 == parity, here, there) for parity in range(2)])
     time = ((iota((2 * LANES, LANES), 1) >> 5) + unit) & 3
     free = ((iota((16, LANES), 1) >> 5) + unit) & 3 == 3
 
     def rows_of(first):
-        return slots_ref[:, first : first + 16, :].reshape(depth, LANES)
+        return slots_ref[:, first // 4 : first // 4 + 4].reshape(depth, LANES)
 
     for p in pairs:
         for j in range(DEVICES // 8):
-            row = jnp.broadcast_to(lines[j][p : p + 1], (16, LANES)).astype(jnp.bfloat16)
+            row = jnp.broadcast_to(lines[j][p & 1][p >> 1 : (p >> 1) + 1], (16, LANES)).astype(jnp.bfloat16)
             row = jnp.concatenate([row] * 16, axis=0)
             select_ref[:, j * LANES : (j + 1) * LANES] = jnp.where(
                 bins == row, jnp.bfloat16(1), jnp.bfloat16(0)
@@ -337,33 +337,34 @@
     vmem = pl.BlockSpec(memory_space=pltpu.VMEM)
     hbm = pl.BlockSpec(memory_space=pltpu.HBM)
     owner_row, cell_row = owner.reshape(1, ROWS), cell.reshape(1, ROWS)
-    out = (N_IN, N_X, CODES + 8, LANES)
+    out = (N_IN, N_X, *BLOCK)
     count = N_X * 16
-    slots, matrix = call(
+    slots = call(
         pack_kernel,
         "pack",
-        (jax.ShapeDtypeStruct(out, bf16), jax.ShapeDtypeStruct((count, count), bf16)),
+        jax.ShapeDtypeStruct(out, bf16),
         [
             pltpu.VMEM((1, ROWS), jnp.int32),
             pltpu.VMEM((1, ROWS), jnp.int32),
-            pltpu.VMEM((1, count), jnp.float32),
-            pltpu.VMEM((count, 2 * count), jnp.float32),
             pltpu.VMEM((CLASSES, SAMPLES), jnp.int32),
             pltpu.VMEM((CLASSES, SAMPLES), jnp.float32),
             pltpu.VMEM((ROWS, SAMPLES), bf16),
-            pltpu.VMEM((count, count), bf16),
             pltpu.VMEM((4, CLASSES, SAMPLES), jnp.int32),
             pltpu.VMEM((ROWS, SAMPLES), bf16),
             pltpu.VMEM((N_IN * SLOTS, ROWS), bf16),
             pltpu.VMEM(out, bf16),
-            dma((7,)),
-            dma((N_IN + 1,)),
+            dma((5,)),
+            dma((N_IN,)),
         ],
-        [hbm] * 7,
-        (hbm, hbm),
+        [hbm] * 5,
+        hbm,
         60,
-    )(owner_row, cell_row, gains.reshape(1, count), jnp.asarray(filter_basis()), shift_table, weight_table, traces)
-    slots = exchange(slots.reshape(DEVICES, CODES + 8, LANES), ("inline", "xline"))
+    )(owner_row, cell_row, shift_table, weight_table, traces)
+    matrix = call(
+        matrix_kernel, "matrix", jax.ShapeDtypeStruct((count, count), bf16), [], [vmem] * 2, vmem, 16
+    )(gains.reshape(1, count), jnp.asarray(filter_basis()))
+    slots = exchange(slots.reshape(DEVICES, *BLOCK), ("inline", "xline"))
+    slots, matrix = lax.optimization_barrier((slots, matrix))
     keep, received = [], []
     for pairs in (range(6), range(6, 8)):
         part = jax.ShapeDtypeStruct((2 * len(pairs), 48, LANES), bf16)

time: 73.4 us -> 72.2 us (0.984)
  blocking collectives: 54.3 us -> 0 us
  waiting for transfers between devices: 2.39 us -> 42.2 us
  starting transfers between devices: 2.17 us -> 13.5 us
  local copies, waits for them, and re-layouts: 0.01 us -> 1.04 us
  Pallas kernels: 13.7 us -> 14.6 us
    all_to_all x1 -> x0, blocking collectives: 54.3 us -> none  [exchange(): return lax.all_to_all(block, axes, split_axis=0, concat_axis=0, tiled=True)]
    all_to_all x0 -> x1, waiting for transfers between devices: none -> 40 us  [exchange(): return lax.all_to_all(block, axes, split_axis=0, concat_axis=0, tiled=True)]
    all_to_all x0 -> x1, starting transfers between devices: none -> 11.1 us  [exchange(): return lax.all_to_all(block, axes, split_axis=0, concat_axis=0, tiled=True)]
    unnamed x2 -> x4, local copies, waits for them, and re-layouts: 0.01 us -> 1.04 us
    pallas_call x1 -> x2, Pallas kernels: 7.31 us -> 7.68 us  [the longest x1 6.98 us: shards(): call(pack_kernel, 'pack', jax.ShapeDtypeStruct(out, bf16), [pltpu.VMEM((1...]
  transfers between devices with their start and end apart: 2 -> 3, of which waited for: 1 -> 2; matrix products, arithmetic and copies ran while one was open for 0% -> 0% of each run, Pallas kernels for 4% -> 5%
where the time goes in v7:
time: 72.2 us; the launch traced here: 71.6 us
  waiting for transfers between devices  42.2 us (58%)
  Pallas kernels  14.6 us (20%)
  starting transfers between devices  13.5 us (19%)
  local copies, waits for them, and re-layouts  1.04 us (1%)
    all_to_all x1, waiting for transfers between devices, exchange(): return lax.all_to_all(block, axes, split_axis=0, concat_axis=0, tiled=True)  40 us
    all_to_all x1, starting transfers between devices, exchange(): return lax.all_to_all(block, axes, split_axis=0, concat_axis=0, tiled=True)  11.1 us
    pallas_call x1, Pallas kernels, shards(): call(pack_kernel, 'pack', jax.ShapeDtypeStruct(out, bf16), [pltpu.VMEM((1...  6.98 us
    pallas_call x2, Pallas kernels, shards(): call(functools.partial(stack_kernel, pairs), f'stack_{pairs[0]}', (part,...  4.64 us
    ppermute x2, starting transfers between devices, shards(): lax.ppermute(send, 'xline', [(x, x ^ 1) for x in range(N_X)])  2.36 us
    ppermute x2, waiting for transfers between devices, shards(): lax.ppermute(send, 'xline', [(x, x ^ 1) for x in range(N_X)])  2.22 us
  transfers between devices with their start and end apart: 3, of which 2 were waited for; matrix products, arithmetic and copies ran while one was open for 0% of the time, Pallas kernels for 5%

profile of v7, /device:TPU:0, one launch (start us, length us, event | category | flops | bytes accessed | tf_op | source)
XLA Modules:
  0.0 71.6 jit_solution(3747590955332239382)
XLA Ops:
  0.0 7.0 %pack.1 = bf16[8,16,25,4,128]{4,3,2,1,0:T(4,128)(2,1)} custom-call(s32[1,512]{1,0:T(1,128)} %bitcast.6, s32[1,512]{1,0:T(1,128)} %bitcast.7, s32[32,1536]{1,0:T(8,128)} %shift_hbm.1, f32[32,1536]{1,0:T(8,128)} %weight_hbm.1, bf16[512,1536]{1,0:T(8,128)(2,1)} %x_hbm.1), custom_call_target="tpu_custom_call" | custom-call | tf_op jit(solution)/shard_map/pack/pallas_call | solution.py:342
  7.0 0.0 copy-start.1
  7.0 11.1 %all-to-all-start = ((bf16[128,25,4,128]{3,2,1,0:T(4,128)(2,1)}), bf16[128,25,4,128]{3,2,1,0:T(4,128)(2,1)S(1)}, u32[]{:S(2)}, u32[]{:S(2)}) async-start(bf16[128,25,4,128]{3,2,1,0:T(4,128)(2,1)} %bitcast.5), calls=%async_computation | async-start | bytes 6553600 | tf_op jit(solution)/shard_map/all_to_all | solution.py:332
  18.2 0.0 copy-done.1
  18.2 0.0 copy-start
  18.2 1.0 %copy-done = f32[256,512]{1,0:T(8,128)S(1)} copy-done((f32[256,512]{1,0:T(8,128)S(1)}, f32[256,512]{1,0:T(8,128)}, u32[]{:S(2)}) %copy-start) | copy-done | bytes 524312
  19.2 0.7 matrix.1.matrix_ref
  19.9 40.0 %all-to-all-done.slots_ref = bf16[128,25,4,128]{3,2,1,0:T(4,128)(2,1)S(1)} async-done(((bf16[128,25,4,128]{3,2,1,0:T(4,128)(2,1)}), bf16[128,25,4,128]{3,2,1,0:T(4,128)(2,1)S(1)}, u32[]{:S(2)}, u32[]{:S(2)}) %all-to-all-start) | async-done | bytes 3276832 | tf_op jit(solution)/shard_map/all_to_all | solution.py:332
  59.9 2.8 %stack_0.1 = (bf16[12,48,128]{2,1,0:T(8,128)(2,1)S(1)}, bf16[12,48,128]{2,1,0:T(8,128)(2,1)S(1)}) custom-call(bf16[128,25,4,128]{3,2,1,0:T(4,128)(2,1)S(1)} %all-to-all-done.slots_ref), custom_call_target="tpu_custom_call" | custom-call | tf_op jit(solution)/shard_map/stack_0/pallas_call | solution.py:371
  62.7 1.6 %collective-permute-start = (bf16[12,48,128]{2,1,0:T(8,128)(2,1)S(1)}, bf16[12,48,128]{2,1,0:T(8,128)(2,1)S(1)}, u32[]{:S(2)}, u32[]{:S(2)}) collective-permute-start(bf16[12,48,128]{2,1,0:T(8,128)(2,1)S(1)} %get-tuple-element.13), channel_id=1, source_target_pairs={{0,1},{1,0},{2,3},{3,2},{4,5},{5,4},{6,7},{7,6},{8,9},{9,8},{10,11... | collective-permute-start | bytes 442376 | tf_op jit(solution)/shard_map/ppermute | solution.py:381
  64.3 1.8 %stack_6.1 = (bf16[4,48,128]{2,1,0:T(8,128)(2,1)S(1)}, bf16[4,48,128]{2,1,0:T(8,128)(2,1)S(1)}) custom-call(bf16[128,25,4,128]{3,2,1,0:T(4,128)(2,1)S(1)} %all-to-all-done.slots_ref), custom_call_target="tpu_custom_call" | custom-call | tf_op jit(solution)/shard_map/stack_6/pallas_call | solution.py:371
  66.1 0.8 %collective-permute-start.1 = (bf16[4,48,128]{2,1,0:T(8,128)(2,1)S(1)}, bf16[4,48,128]{2,1,0:T(8,128)(2,1)S(1)}, u32[]{:S(2)}, u32[]{:S(2)}) collective-permute-start(bf16[4,48,128]{2,1,0:T(8,128)(2,1)S(1)} %get-tuple-element.14), channel_id=1, source_target_pairs={{0,1},{1,0},{2,3},{3,2},{4,5},{5,4},{6,7},{7,6},{8,9},{9,8},{10,11... | collective-permute-start | bytes 147464 | tf_op jit(solution)/shard_map/ppermute | solution.py:381
  66.9 1.2 %crossline_own.1.rest_0_ = f32[192,4,256]{2,1,0:T(4,128)} custom-call(bf16[256,256]{1,0:T(8,128)(2,1)S(1)} %matrix.1.matrix_ref, bf16[12,48,128]{2,1,0:T(8,128)(2,1)S(1)} %get-tuple-element.15.first_ref, bf16[4,48,128]{2,1,0:T(8,128)(2,1)S(1)} %get-tuple-element.16.second_ref), custom_call_target="tpu_custom_call" | custom-call | tf_op jit(solution)/shard_map/crossline_own/pallas_call | solution.py:384
  68.1 2.2 %collective-permute-done.1.second_ref = bf16[4,48,128]{2,1,0:T(8,128)(2,1)S(1)} collective-permute-done((bf16[4,48,128]{2,1,0:T(8,128)(2,1)S(1)}, bf16[4,48,128]{2,1,0:T(8,128)(2,1)S(1)}, u32[]{:S(2)}, u32[]{:S(2)}) %collective-permute-start.1) | collective-permute-done | bytes 49184 | tf_op jit(solution)/shard_map/ppermute | solution.py:381
  70.3 0.0 collective-permute-done.first_ref
  70.3 1.2 %crossline_received.1 = f32[192,4,256]{2,1,0:T(4,128)} custom-call(bf16[256,256]{1,0:T(8,128)(2,1)S(1)} %matrix.1.matrix_ref, bf16[12,48,128]{2,1,0:T(8,128)(2,1)S(1)} %collective-permute-done.first_ref, bf16[4,48,128]{2,1,0:T(8,128)(2,1)S(1)} %collective-permute-done.1.second_ref, f32[192,4,256]{2,1,0:T(4,128)} %crossline_own.1.rest_0_), custom_call_target="tpu_custom_call", output_to_operand_aliasing={{}: (3, {})} | custom-call | tf_op jit(solution)/shard_map/crossline_received/pallas_call | solution.py:387
Async XLA Ops:
  7.0 11.2 %copy-start.1 = (f32[256]{0:T(256)S(1)}, f32[256]{0:T(256)}, u32[]{:S(2)}) copy-start(f32[256]{0:T(256)} %param.12) | copy-start | bytes 3076
  7.0 52.9 %all-to-all-start = ((bf16[128,25,4,128]{3,2,1,0:T(4,128)(2,1)}), bf16[128,25,4,128]{3,2,1,0:T(4,128)(2,1)S(1)}, u32[]{:S(2)}, u32[]{:S(2)}) async-start(bf16[128,25,4,128]{3,2,1,0:T(4,128)(2,1)} %bitcast.5), calls=%async_computation | async-start | bytes 6553600 | tf_op jit(solution)/shard_map/all_to_all | solution.py:332
  18.2 1.0 %copy-start = (f32[256,512]{1,0:T(8,128)S(1)}, f32[256,512]{1,0:T(8,128)}, u32[]{:S(2)}) copy-start(f32[256,512]{1,0:T(8,128)} %constant.2.clone.basis_ref) | copy-start | bytes 1572868
  62.7 7.6 %collective-permute-start = (bf16[12,48,128]{2,1,0:T(8,128)(2,1)S(1)}, bf16[12,48,128]{2,1,0:T(8,128)(2,1)S(1)}, u32[]{:S(2)}, u32[]{:S(2)}) collective-permute-start(bf16[12,48,128]{2,1,0:T(8,128)(2,1)S(1)} %get-tuple-element.13), channel_id=1, source_target_pairs={{0,1},{1,0},{2,3},{3,2},{4,5},{5,4},{6,7},{7,6},{8,9},{9,8},{10,11... | collective-permute-start | bytes 442376 | tf_op jit(solution)/shard_map/ppermute | solution.py:381
  66.1 4.2 %collective-permute-start.1 = (bf16[4,48,128]{2,1,0:T(8,128)(2,1)S(1)}, bf16[4,48,128]{2,1,0:T(8,128)(2,1)S(1)}, u32[]{:S(2)}, u32[]{:S(2)}) collective-permute-start(bf16[4,48,128]{2,1,0:T(8,128)(2,1)S(1)} %get-tuple-element.14), channel_id=1, source_target_pairs={{0,1},{1,0},{2,3},{3,2},{4,5},{5,4},{6,7},{7,6},{8,9},{9,8},{10,11... | collective-permute-start | bytes 147464 | tf_op jit(solution)/shard_map/ppermute | solution.py:381

commit v8 on v7

--- a/solution.py
+++ b/solution.py
@@ -141,7 +141,7 @@
     slot = slot_of_rows(owner_ref[...])
     spread(slot, place_ref)
     arrivals[1].wait()
-    code = ((slot >> 3) & 1) * LANES + cell_ref[...] + 1
+    code = cell_ref[...] + 1
     lines = N_IN * 4
     held = jnp.where(iota((lines, ROWS), 0) == slot >> 5, code.astype(jnp.float32), 0.0).astype(jnp.bfloat16)
     lanes = jnp.where((iota((LANES, ROWS), 0) & 31) == (slot & 31), 1.0, 0.0).astype(jnp.bfloat16)
@@ -151,8 +151,10 @@
     for x in range(N_X):
         for i in range(N_IN):
             out_ref[i, x, CODES] = codes[x // 2]
-    for copy in arrivals[2:]:
-        copy.wait()
+    arrivals[2].wait()
+    narrow = table_places(shift_ref, places_ref)
+    arrivals[3].wait()
+    arrivals[4].wait()
     chunk = iota((CHUNK, LANES), 1) >> 5
 
     def place(n):
@@ -212,7 +214,6 @@
         for n in range(TILES // 3):
             place(n)
 
-    narrow = table_places(shift_ref, places_ref)
     pl.when(narrow)(lambda: all_tiles(True))
     pl.when(jnp.logical_not(narrow))(lambda: all_tiles(False))
     for copy in departures:
@@ -225,31 +226,37 @@
     return half, first + half, first + 1 - half
 
 
-def stack_kernel(pairs, slots_ref, keep_ref, send_ref, select_ref, halves_ref):
+def stack_kernel(owners, slots_ref, keep_ref, send_ref, select_ref, halves_ref):
     half, unit, _ = units()
-    bins = (iota((2 * LANES, LANES), 0) + 1).astype(jnp.float32).astype(jnp.bfloat16)
-    depth = DEVICES * 16
+    bins = (iota((LANES, LANES), 0) + 1).astype(jnp.float32).astype(jnp.bfloat16)
+    depth = DEVICES * 8
     ones = jnp.ones((depth, LANES), jnp.bfloat16)
-    group = iota((4, LANES), 1) >> 4
+    group = iota((4, LANES), 1) >> 3
+    at = [group == g for g in range(16)]
+    apart = [[((group - c) & 3) == d for d in range(4)] for c in range(4)]
     lines = []
-    for j in range(DEVICES // 8):
-        here = there = jnp.zeros((4, LANES), jnp.float32)
-        for g in range(8):
-            codes = slots_ref[8 * j + g, CODES].astype(jnp.float32)
-            here = jnp.where(group == g, codes, here)
-            there = jnp.where(group == (g - 1) % 8, codes, there)
-        there = pltpu.roll(there, 16, 1)
-        lines.append([jnp.where(group & 1 == parity, here, there) for parity in range(2)])
-    time = ((iota((2 * LANES, LANES), 1) >> 5) + unit) & 3
+    for j in range(DEVICES // 16):
+        turned = [jnp.zeros((4, LANES), jnp.float32) for _ in range(4)]
+        for g in range(16):
+            codes = slots_ref[16 * j + g, CODES].astype(jnp.float32)
+            turned = [jnp.where(at[(g - d) % 16], codes, turned[d]) for d in range(4)]
+        turned = [turned[0]] + [pltpu.roll(turned[d], 8 * d, 1) for d in range(1, 4)]
+        lines.append([])
+        for c in range(4):
+            line = turned[0]
+            for d in range(1, 4):
+                line = jnp.where(apart[c][d], turned[d], line)
+            lines[j].append(line)
+    time = ((iota((LANES, LANES), 1) >> 5) + unit) & 3
     free = ((iota((16, LANES), 1) >> 5) + unit) & 3 == 3
 
     def rows_of(first):
-        return slots_ref[:, first // 4 : first // 4 + 4].reshape(depth, LANES)
-
-    for p in pairs:
-        for j in range(DEVICES // 8):
-            row = jnp.broadcast_to(lines[j][p & 1][p >> 1 : (p >> 1) + 1], (16, LANES)).astype(jnp.bfloat16)
-            row = jnp.concatenate([row] * 16, axis=0)
+        return slots_ref[:, first // 4 : first // 4 + 2].reshape(depth, LANES)
+
+    for o in owners:
+        for j in range(DEVICES // 16):
+            row = jnp.broadcast_to(lines[j][o % 4][o // 4 : o // 4 + 1], (16, LANES)).astype(jnp.bfloat16)
+            row = jnp.concatenate([row] * 8, axis=0)
             select_ref[:, j * LANES : (j + 1) * LANES] = jnp.where(
                 bins == row, jnp.bfloat16(1), jnp.bfloat16(0)
             )
@@ -259,23 +266,22 @@
             both = jnp.dot(select, jnp.concatenate([a, b], axis=1), preferred_element_type=jnp.float32)
             return both[:, :LANES], both[:, LANES:]
 
-        if p < 6:
-            sums, fold = sums_of(rows_of(16 * p), ones)
+        if o < 12:
+            sums, fold = sums_of(rows_of(8 * o), ones)
         else:
-            first, second = sums_of(rows_of(16 * (p - 6)), rows_of(CHUNK + 16 * (p - 6)))
-            third, fold = sums_of(rows_of(2 * CHUNK + 16 * (p - 6)), ones)
+            first, second = sums_of(rows_of(8 * (o - 12)), rows_of(CHUNK + 8 * (o - 12)))
+            third, fold = sums_of(rows_of(2 * CHUNK + 8 * (o - 12)), ones)
             first, second, third = (
                 pltpu.roll(part, CHUNK * (q + 1), 1) for q, part in enumerate((first, second, third))
             )
             sums = jnp.where(time == 0, first, jnp.where(time == 1, second, third))
         mean = sums / jnp.maximum(fold, 1.0)
-        for o in range(2):
-            for h in range(2):
-                four = [mean[o * LANES + h * 64 + 16 * i : o * LANES + h * 64 + 16 * i + 16] for i in range(4)]
-                for i in range(3):
-                    halves_ref[h, 2 * (p - pairs[0]) + o, 16 * i : 16 * i + 16, :] = jnp.where(
-                        free, pltpu.roll(four[3], CHUNK * (3 - i), 1), four[i]
-                    ).astype(jnp.bfloat16)
+        for h in range(2):
+            four = [mean[h * 64 + 16 * i : h * 64 + 16 * i + 16] for i in range(4)]
+            for i in range(3):
+                halves_ref[h, o - owners[0], 16 * i : 16 * i + 16, :] = jnp.where(
+                    free, pltpu.roll(four[3], CHUNK * (3 - i), 1), four[i]
+                ).astype(jnp.bfloat16)
     send_ref[...] = halves_ref[1 - half]
     keep_ref[...] = halves_ref[half]
 
@@ -366,13 +372,13 @@
     slots = exchange(slots.reshape(DEVICES, *BLOCK), ("inline", "xline"))
     slots, matrix = lax.optimization_barrier((slots, matrix))
     keep, received = [], []
-    for pairs in (range(6), range(6, 8)):
-        part = jax.ShapeDtypeStruct((2 * len(pairs), 48, LANES), bf16)
+    for owners in (range(12), range(12, 16)):
+        part = jax.ShapeDtypeStruct((len(owners), 48, LANES), bf16)
         kept, send = call(
-            functools.partial(stack_kernel, pairs),
-            f"stack_{pairs[0]}",
+            functools.partial(stack_kernel, owners),
+            f"stack_{owners[0]}",
             (part, part),
-            [pltpu.VMEM((2 * LANES, DEVICES * 16), bf16), pltpu.VMEM((2, *part.shape), bf16)],
+            [pltpu.VMEM((LANES, DEVICES * 8), bf16), pltpu.VMEM((2, *part.shape), bf16)],
             [vmem],
             (vmem, vmem),
             32,

time: 72.2 us -> 70.9 us (0.982)
  Pallas kernels: 14.6 us -> 13.2 us
    pallas_call x2, Pallas kernels: 4.64 us -> 3.45 us  [shards(): call(functools.partial(stack_kernel, owners), f'stack_{owners[0]}', (part...]
where the time goes in v8:
time: 70.9 us; the launch traced here: 70.2 us
  waiting for transfers between devices  42.5 us (60%)
  starting transfers between devices  13.3 us (19%)
  Pallas kernels  13.2 us (19%)
  local copies, waits for them, and re-layouts  1.04 us (1%)
    all_to_all x1, waiting for transfers between devices, exchange(): return lax.all_to_all(block, axes, split_axis=0, concat_axis=0, tiled=True)  40 us
    all_to_all x1, starting transfers between devices, exchange(): return lax.all_to_all(block, axes, split_axis=0, concat_axis=0, tiled=True)  11.1 us
    pallas_call x1, Pallas kernels, shards(): call(pack_kernel, 'pack', jax.ShapeDtypeStruct(out, bf16), [pltpu.VMEM((1...  6.76 us
    pallas_call x2, Pallas kernels, shards(): call(functools.partial(stack_kernel, owners), f'stack_{owners[0]}', (part...  3.45 us
    ppermute x2, waiting for transfers between devices, shards(): lax.ppermute(send, 'xline', [(x, x ^ 1) for x in range(N_X)])  2.55 us
    ppermute x2, starting transfers between devices, shards(): lax.ppermute(send, 'xline', [(x, x ^ 1) for x in range(N_X)])  2.19 us
  transfers between devices with their start and end apart: 3, of which 2 were waited for; matrix products, arithmetic and copies ran while one was open for 0% of the time, Pallas kernels for 5%

profile of v8, /device:TPU:0, one launch (start us, length us, event | category | flops | bytes accessed | tf_op | source)
XLA Modules:
  0.0 70.2 jit_solution(7125133239694366185)
XLA Ops:
  0.0 6.8 %pack.1 = bf16[8,16,25,4,128]{4,3,2,1,0:T(4,128)(2,1)} custom-call(s32[1,512]{1,0:T(1,128)} %bitcast.6, s32[1,512]{1,0:T(1,128)} %bitcast.7, s32[32,1536]{1,0:T(8,128)} %shift_hbm.1, f32[32,1536]{1,0:T(8,128)} %weight_hbm.1, bf16[512,1536]{1,0:T(8,128)(2,1)} %x_hbm.1), custom_call_target="tpu_custom_call" | custom-call | tf_op jit(solution)/shard_map/pack/pallas_call | solution.py:348
  6.8 0.0 copy-start.1
  6.8 11.1 %all-to-all-start = ((bf16[128,25,4,128]{3,2,1,0:T(4,128)(2,1)}), bf16[128,25,4,128]{3,2,1,0:T(4,128)(2,1)S(1)}, u32[]{:S(2)}, u32[]{:S(2)}) async-start(bf16[128,25,4,128]{3,2,1,0:T(4,128)(2,1)} %bitcast.5), calls=%async_computation | async-start | bytes 6553600 | tf_op jit(solution)/shard_map/all_to_all | solution.py:338
  17.9 0.0 copy-done.1
  18.0 0.0 copy-start
  18.0 1.0 %copy-done = f32[256,512]{1,0:T(8,128)S(1)} copy-done((f32[256,512]{1,0:T(8,128)S(1)}, f32[256,512]{1,0:T(8,128)}, u32[]{:S(2)}) %copy-start) | copy-done | bytes 524312
  19.0 0.7 matrix.1.matrix_ref
  19.7 40.0 %all-to-all-done.slots_ref = bf16[128,25,4,128]{3,2,1,0:T(4,128)(2,1)S(1)} async-done(((bf16[128,25,4,128]{3,2,1,0:T(4,128)(2,1)}), bf16[128,25,4,128]{3,2,1,0:T(4,128)(2,1)S(1)}, u32[]{:S(2)}, u32[]{:S(2)}) %all-to-all-start) | async-done | bytes 3276832 | tf_op jit(solution)/shard_map/all_to_all | solution.py:338
  59.7 2.1 %stack_0.1 = (bf16[12,48,128]{2,1,0:T(8,128)(2,1)S(1)}, bf16[12,48,128]{2,1,0:T(8,128)(2,1)S(1)}) custom-call(bf16[128,25,4,128]{3,2,1,0:T(4,128)(2,1)S(1)} %all-to-all-done.slots_ref), custom_call_target="tpu_custom_call" | custom-call | tf_op jit(solution)/shard_map/stack_0/pallas_call | solution.py:377
  61.8 1.4 %collective-permute-start = (bf16[12,48,128]{2,1,0:T(8,128)(2,1)S(1)}, bf16[12,48,128]{2,1,0:T(8,128)(2,1)S(1)}, u32[]{:S(2)}, u32[]{:S(2)}) collective-permute-start(bf16[12,48,128]{2,1,0:T(8,128)(2,1)S(1)} %get-tuple-element.13), channel_id=1, source_target_pairs={{0,1},{1,0},{2,3},{3,2},{4,5},{5,4},{6,7},{7,6},{8,9},{9,8},{10,11... | collective-permute-start | bytes 442376 | tf_op jit(solution)/shard_map/ppermute | solution.py:387
  63.2 1.4 %stack_12.1 = (bf16[4,48,128]{2,1,0:T(8,128)(2,1)S(1)}, bf16[4,48,128]{2,1,0:T(8,128)(2,1)S(1)}) custom-call(bf16[128,25,4,128]{3,2,1,0:T(4,128)(2,1)S(1)} %all-to-all-done.slots_ref), custom_call_target="tpu_custom_call" | custom-call | tf_op jit(solution)/shard_map/stack_12/pallas_call | solution.py:377
  64.6 0.8 %collective-permute-start.1 = (bf16[4,48,128]{2,1,0:T(8,128)(2,1)S(1)}, bf16[4,48,128]{2,1,0:T(8,128)(2,1)S(1)}, u32[]{:S(2)}, u32[]{:S(2)}) collective-permute-start(bf16[4,48,128]{2,1,0:T(8,128)(2,1)S(1)} %get-tuple-element.14), channel_id=1, source_target_pairs={{0,1},{1,0},{2,3},{3,2},{4,5},{5,4},{6,7},{7,6},{8,9},{9,8},{10,11... | collective-permute-start | bytes 147464 | tf_op jit(solution)/shard_map/ppermute | solution.py:387
  65.3 1.2 %crossline_own.1.rest_0_ = f32[192,4,256]{2,1,0:T(4,128)} custom-call(bf16[256,256]{1,0:T(8,128)(2,1)S(1)} %matrix.1.matrix_ref, bf16[12,48,128]{2,1,0:T(8,128)(2,1)S(1)} %get-tuple-element.15.first_ref, bf16[4,48,128]{2,1,0:T(8,128)(2,1)S(1)} %get-tuple-element.16.second_ref), custom_call_target="tpu_custom_call" | custom-call | tf_op jit(solution)/shard_map/crossline_own/pallas_call | solution.py:390
  66.5 2.5 %collective-permute-done.1.second_ref = bf16[4,48,128]{2,1,0:T(8,128)(2,1)S(1)} collective-permute-done((bf16[4,48,128]{2,1,0:T(8,128)(2,1)S(1)}, bf16[4,48,128]{2,1,0:T(8,128)(2,1)S(1)}, u32[]{:S(2)}, u32[]{:S(2)}) %collective-permute-start.1) | collective-permute-done | bytes 49184 | tf_op jit(solution)/shard_map/ppermute | solution.py:387
  69.0 0.0 collective-permute-done.first_ref
  69.0 1.2 %crossline_received.1 = f32[192,4,256]{2,1,0:T(4,128)} custom-call(bf16[256,256]{1,0:T(8,128)(2,1)S(1)} %matrix.1.matrix_ref, bf16[12,48,128]{2,1,0:T(8,128)(2,1)S(1)} %collective-permute-done.first_ref, bf16[4,48,128]{2,1,0:T(8,128)(2,1)S(1)} %collective-permute-done.1.second_ref, f32[192,4,256]{2,1,0:T(4,128)} %crossline_own.1.rest_0_), custom_call_target="tpu_custom_call", output_to_operand_aliasing={{}: (3, {})} | custom-call | tf_op jit(solution)/shard_map/crossline_received/pallas_call | solution.py:393
Async XLA Ops:
  6.8 11.2 %copy-start.1 = (f32[256]{0:T(256)S(1)}, f32[256]{0:T(256)}, u32[]{:S(2)}) copy-start(f32[256]{0:T(256)} %param.12) | copy-start | bytes 3076
  6.8 52.9 %all-to-all-start = ((bf16[128,25,4,128]{3,2,1,0:T(4,128)(2,1)}), bf16[128,25,4,128]{3,2,1,0:T(4,128)(2,1)S(1)}, u32[]{:S(2)}, u32[]{:S(2)}) async-start(bf16[128,25,4,128]{3,2,1,0:T(4,128)(2,1)} %bitcast.5), calls=%async_computation | async-start | bytes 6553600 | tf_op jit(solution)/shard_map/all_to_all | solution.py:338
  18.0 1.0 %copy-start = (f32[256,512]{1,0:T(8,128)S(1)}, f32[256,512]{1,0:T(8,128)}, u32[]{:S(2)}) copy-start(f32[256,512]{1,0:T(8,128)} %constant.2.clone.basis_ref) | copy-start | bytes 1572868
  61.8 7.3 %collective-permute-start = (bf16[12,48,128]{2,1,0:T(8,128)(2,1)S(1)}, bf16[12,48,128]{2,1,0:T(8,128)(2,1)S(1)}, u32[]{:S(2)}, u32[]{:S(2)}) collective-permute-start(bf16[12,48,128]{2,1,0:T(8,128)(2,1)S(1)} %get-tuple-element.13), channel_id=1, source_target_pairs={{0,1},{1,0},{2,3},{3,2},{4,5},{5,4},{6,7},{7,6},{8,9},{9,8},{10,11... | collective-permute-start | bytes 442376 | tf_op jit(solution)/shard_map/ppermute | solution.py:387
  64.6 4.5 %collective-permute-start.1 = (bf16[4,48,128]{2,1,0:T(8,128)(2,1)S(1)}, bf16[4,48,128]{2,1,0:T(8,128)(2,1)S(1)}, u32[]{:S(2)}, u32[]{:S(2)}) collective-permute-start(bf16[4,48,128]{2,1,0:T(8,128)(2,1)S(1)} %get-tuple-element.14), channel_id=1, source_target_pairs={{0,1},{1,0},{2,3},{3,2},{4,5},{5,4},{6,7},{7,6},{8,9},{9,8},{10,11... | collective-permute-start | bytes 147464 | tf_op jit(solution)/shard_map/ppermute | solution.py:387
